TPU v7x, 256 devices: a whole 4x4x8 slice. The times are simulated.
256 devices in a mesh: pts: 8 (over z), cent: 32 (over x, y, core).
Axes of the slice: x: 4, y: 4, z: 8, core: 2. Of those that a mesh axis runs over, the one named last changes fastest.
Arguments:
- points: bfloat16 [8192, 1024], P('pts', 'cent'), may hold values from -1 to 1, as said below
- centroids: bfloat16 [65536, 1024], P('cent'), may hold values from -1.25 to 1.25, as said below
Outputs:
- grad_points: float32 [8192, 1024], P('pts', 'cent')
- grad_centroids: float32 [65536, 1024], P('cent', 'pts')
- loss: float32 [], replicated
Inputs may be any that keep to these rules, and one draw needn't show every extreme that they name: centroids are independent rows with scales spread over a range. `points`: each point lies near a scaled centroid.
All inputs are finite; a program needn't handle non-finite values.
Results may differ from a plain program's by a relative error of at most 0.0003.
Values may be sent and summed in bfloat16 or wider, within the bound.
No kernel may reach another device: no remote copies, remote signals or barrier semaphores. Data moves between devices by JAX's collectives and lax.ppermute only.
A program may use at most 256 MiB of HBM per device.

v0:
```python
import jax
import jax.numpy as jnp
from jax import lax
from jax.sharding import PartitionSpec as P


def per_device(points, centroids):
    zrows = lax.all_gather(points, "cent", axis=1, tiled=True)
    rows = zrows.shape[0]
    local_cent = centroids.shape[0]
    total = rows * lax.axis_size("pts")
    clusters = local_cent * lax.axis_size("cent")
    scale = 2.0 * clusters / total
    zfloat = zrows.astype(jnp.float32)
    zsq = jnp.sum(zfloat * zfloat, axis=1)
    cfloat = centroids.astype(jnp.float32)
    msq = jnp.sum(cfloat * cfloat, axis=1)
    dots = jnp.einsum("pd,kd->pk", zrows, centroids, preferred_element_type=jnp.float32)
    kern = 1.0 / (1.0 + zsq[:, None] + msq[None, :] - 2.0 * dots)
    norm = lax.psum(jnp.sum(kern, axis=1), "cent")
    soft = kern / norm[:, None]
    freq = lax.psum(jnp.sum(soft, axis=0), "pts")
    sharp = soft * soft / freq[None, :]
    denom = lax.psum(jnp.sum(sharp, axis=1), "cent")
    target = sharp / denom[:, None]
    kl_part = jnp.sum(target * jnp.log(target / soft))
    kl_sum = lax.psum(kl_part, ("pts", "cent"))
    coef = kern * (target - soft)
    term_points = jnp.sum(coef, axis=1)[:, None] * zfloat - jnp.dot(
        coef, cfloat, precision=lax.Precision.HIGHEST
    )
    summed = lax.psum_scatter(term_points, "cent", scatter_dimension=1, tiled=True)
    grad_points = scale * summed
    term_cent = (
        jnp.dot(coef.T, zfloat, precision=lax.Precision.HIGHEST)
        - jnp.sum(coef, axis=0)[:, None] * cfloat
    )
    part = lax.psum_scatter(term_cent, "pts", scatter_dimension=1, tiled=True)
    grad_centroids = -scale * part
    return (grad_points, grad_centroids, kl_sum / total)


def solution(mesh):
    in_specs = (P("pts", "cent"), P("cent", None))
    out_specs = (P("pts", "cent"), P("cent", "pts"), P())
    return jax.shard_map(
        per_device, mesh=mesh, in_specs=in_specs, out_specs=out_specs, check_vma=False
    )
```

profile of v0, /device:TPU:8, one launch (start us, length us, event | category | flops | bytes accessed | tf_op | source)
XLA Modules:
  0.0 452.1 jit_solution(4664661445842199192)
XLA Ops:
  7.2 0.0 all-gather.2.cloned.1.call-start
  7.2 0.7 all-gather.2.cloned.1.call-update
  7.9 0.0 reduce-scatter.3.cloned.1.call-start
  7.9 3.1 fusion
  11.0 50.8 %all-gather.2.cloned.1.call-done = bf16[1024,1024]{0,1:T(8,128)(2,1)} async-done(((bf16[1024,32]{0,1:T(8,128)(2,1)}), bf16[1024,1024]{0,1:T(8,128)(2,1)}) %all-gather.2.cloned.1.call-update) | async-done | bytes 2097168 | tf_op jit(solution)/shard_map/all_gather | solution.py:8
  61.9 2.1 fusion.6
  63.9 11.9 %fusion.8 = (f32[1024]{0:T(1024)S(1)}, f32[1024,2048]{1,0:T(8,128)}) fusion(f32[2048]{0:T(1024)S(1)} %fusion, f32[1024]{0:T(1024)S(1)} %broadcast_add_fusion, bf16[1024,1024]{0,1:T(8,128)(2,1)} %all-gather.2.cloned.1.call-done, bf16[2048,1024]{1,0:T(8,128)(2,1)} %param.3), kind=kOutput, calls=%fused_computation.21 | convolution fusion | flops 4305452032 | bytes 14696448 | tf_op jit(solution)/shard_map/pd,kd->pk/dot_general | solution.py:18
  75.9 60.6 %psum.28 = f32[1024]{0:T(1024)S(1)} all-reduce(f32[1024]{0:T(1024)S(1)} %get-tuple-element.9), channel_id=1, replica_groups=mesh['pts'=8,'cent'=32] {'cent'}, use_global_device_ids=true, to_apply=%region_3.0 | all-reduce | flops 1024 | bytes 8192 | tf_op jit(solution)/shard_map/psum | solution.py:20
  136.5 6.4 %fusion.10 = (f32[2048]{0:T(1024)S(1)}, f32[1024,2048]{1,0:T(8,128)}) fusion(f32[1024]{0:T(1024)S(1)} %psum.28, f32[1024,2048]{1,0:T(8,128)} %get-tuple-element.10, f32[2048]{0:T(1024)S(1)} %fusion, f32[1024]{0:T(1024)S(1)} %broadcast_add_fusion), kind=kLoop, calls=%fused_computation.23 | loop fusion | flops 12580864 | bytes 16801792 | tf_op jit(solution)/shard_map/reduce_sum | solution.py:22
  142.9 17.7 %psum.29 = f32[2048]{0:T(1024)S(1)} all-reduce(f32[2048]{0:T(1024)S(1)} %get-tuple-element.6), channel_id=1, replica_groups=mesh['pts'=8,'cent'=32] {'pts'}, use_global_device_ids=true, to_apply=%region_5.0 | all-reduce | flops 2048 | bytes 16384 | tf_op jit(solution)/shard_map/psum | solution.py:22
  160.6 4.3 divide_reduce_fusion
  164.8 62.8 %psum.30 = f32[1024]{0:T(1024)S(1)} all-reduce(f32[1024]{0:T(1024)S(1)} %divide_reduce_fusion), channel_id=1, replica_groups=mesh['pts'=8,'cent'=32] {'cent'}, use_global_device_ids=true, to_apply=%region_7.0 | all-reduce | flops 1024 | bytes 8192 | tf_op jit(solution)/shard_map/psum | solution.py:24
  227.7 0.0 copy-start.1
  227.7 0.0 copy-start.2
  227.7 10.6 %fusion.9 = (f32[2048]{0:T(1024)S(1)}, f32[1024]{0:T(1024)S(1)}, f32[1024,2048]{1,0:T(8,128)S(1)}, f32[]{:T(128)}) fusion(f32[1024,2048]{1,0:T(8,128)} %get-tuple-element.7, f32[1024]{0:T(1024)S(1)} %psum.30, f32[2048]{0:T(1024)S(1)} %psum.29, f32[1024,2048]{1,0:T(8,128)} %get-tuple-element.10, f32[2048]{0:T(1024)S(1)} %fusion, ...), kind=kLoop, calls=%fused_computation.22 | loop fusion | flops 33551360 | bytes 25206788 | tf_op jit(solution)/shard_map/reduce_sum | solution.py:36
  238.3 0.0 copy-start
  238.3 3.2 copy-done
  241.5 0.0 copy-done.1
  241.5 0.0 copy-done.2
  241.5 15.0 %fusion.7 = f32[1024,1024]{0,1:T(8,128)} fusion(bf16[1024,1024]{0,1:T(8,128)(2,1)S(1)} %copy-done.2, f32[1024]{0:T(1024)S(1)} %get-tuple-element.4, f32[1024,2048]{1,0:T(8,128)S(1)} %get-tuple-element.5, bf16[2048,1024]{1,0:T(8,128)(2,1)S(1)} %copy-done.1), kind=kOutput, calls=%fused_computation.17 | convolution fusion | flops 25772949504 | bytes 18878464 | tf_op jit(solution)/shard_map/dot_general | solution.py:29
  256.5 0.0 reduce-scatter.3.cloned.1.call-update
  256.5 0.3 reduce-scatter.5.cloned.1.call-start
  256.7 30.9 %fusion.1 = f32[2048,1024]{1,0:T(8,128)} fusion(bf16[2048,1024]{1,0:T(8,128)(2,1)} %param.3, f32[2048]{0:T(1024)S(1)} %get-tuple-element.3, f32[1024,2048]{1,0:T(8,128)} %copy-done, bf16[1024,1024]{0,1:T(8,128)(2,1)S(1)} %copy-done.2), kind=kOutput, calls=%fused_computation.5 | convolution fusion | flops 25776095232 | bytes 23076864 | tf_op jit(solution)/shard_map/dot_general | solution.py:35
  287.6 0.0 reduce-scatter.5.cloned.1.call-update
  287.7 76.3 %psum.31 = f32[]{:T(128)} all-reduce(f32[]{:T(128)} %get-tuple-element.8), channel_id=1, replica_groups=mesh['pts'=8,'cent'=32] {'pts','cent'}, use_global_device_ids=true, to_apply=%region_13.0 | all-reduce | flops 1 | bytes 8 | tf_op jit(solution)/shard_map/psum | solution.py:27
  364.6 0.0 reduce-scatter.3.cloned.1.call-done
  364.7 1.6 broadcast_multiply_fusion.1
  366.2 75.9 %reduce-scatter.5.cloned.1.call-done = f32[2048,128]{1,0:T(8,128)} async-done(((f32[2048,1024]{1,0:T(8,128)}), f32[2048,128]{1,0:T(8,128)}) %reduce-scatter.5.cloned.1.call-update) | async-done | bytes 1048592 | tf_op jit(solution)/shard_map/reduce_scatter | solution.py:38
  442.1 2.3 broadcast_multiply_fusion
  (1 shorter events, 0.0 us)
Async XLA Ops:
  7.2 54.7 %all-gather.2.cloned.1.call-start = ((), (), s32[]{:S(2)}) async-start(), calls=%async_computation.2 | async-start | bytes 2162688 | tf_op jit(solution)/shard_map/all_gather | solution.py:8
  7.9 356.8 %reduce-scatter.3.cloned.1.call-start = ((), (), s32[]{:S(2)}) async-start(), calls=%async_computation.3 | async-start | bytes 4325376 | tf_op jit(solution)/shard_map/reduce_scatter | solution.py:32
  227.7 13.8 %copy-start.1 = (bf16[2048,1024]{1,0:T(8,128)(2,1)S(1)}, bf16[2048,1024]{1,0:T(8,128)(2,1)}, u32[]{:S(2)}) copy-start(bf16[2048,1024]{1,0:T(8,128)(2,1)} %param.3) | copy-start | bytes 12582916
  227.7 13.8 %copy-start.2 = (bf16[1024,1024]{0,1:T(8,128)(2,1)S(1)}, bf16[1024,1024]{0,1:T(8,128)(2,1)}, u32[]{:S(2)}) copy-start(bf16[1024,1024]{0,1:T(8,128)(2,1)} %all-gather.2.cloned.1.call-done) | copy-start | bytes 6291460
  238.3 3.2 copy-start
  256.5 185.7 %reduce-scatter.5.cloned.1.call-start = ((), (), s32[]{:S(2)}) async-start(), calls=%async_computation.4 | async-start | bytes 9437184 | tf_op jit(solution)/shard_map/reduce_scatter | solution.py:38
Sparse Core Ops, SparseCore 0:
  10.6 51.2 all-gather.1
  256.6 88.1 reduce-scatter.2
  347.5 94.5 reduce-scatter.4
where the time goes:
time: 453 us; the launch traced here: 452 us
  blocking collectives  217 us (48%)
  waiting for transfers between devices  127 us (28%)
  matrix products  57.8 us (13%)
  other arithmetic  30.2 us (7%)
  between operations  15.6 us (3%)
    psum x1, blocking collectives, per_device(): kl_sum = lax.psum(kl_part, ('pts', 'cent'))  76.3 us
    reduce_scatter x1, waiting for transfers between devices, per_device(): part = lax.psum_scatter(term_cent, 'pts', scatter_dimension=1, tiled=True)  75.9 us
    psum x1, blocking collectives, per_device(): denom = lax.psum(jnp.sum(sharp, axis=1), 'cent')  62.8 us
    psum x1, blocking collectives, per_device(): norm = lax.psum(jnp.sum(kern, axis=1), 'cent')  60.6 us
    all_gather x1, waiting for transfers between devices, per_device(): zrows = lax.all_gather(points, 'cent', axis=1, tiled=True)  50.8 us
    dot_general x1, matrix products, per_device(): jnp.dot(coef.T, zfloat, precision=lax.Precision.HIGHEST)  30.9 us
    psum x1, blocking collectives, per_device(): freq = lax.psum(jnp.sum(soft, axis=0), 'pts')  17.7 us
    dot_general x1, matrix products, per_device(): jnp.dot(coef, cfloat, precision=lax.Precision.HIGHEST)  15 us
  transfers between devices with their start and end apart: 3, of which 2 were waited for; matrix products, arithmetic and copies ran while one was open for 8% of the time, Pallas kernels for 0%

commit v1 on v0

v1 whole, which is shorter than its diff:
```python
import jax
import jax.numpy as jnp
from jax import lax
from jax.sharding import PartitionSpec as P

NX, NY, NC, NZ = 4, 4, 2, 8


def cent_id(x, y, c):
    return (x * NY + y) * NC + c


def cent_shift(dx, dy, dc):
    pairs = []
    for x in range(NX):
        for y in range(NY):
            for c in range(NC):
                src = cent_id(x, y, c)
                dst = cent_id((x + dx) % NX, (y + dy) % NY, c ^ dc)
                pairs.append((src, dst))
    return pairs


def z_shift(k):
    return [(i, (i + k) % NZ) for i in range(NZ)]


def sum_over(v, axis, n):
    w = jnp.broadcast_to(v[None], (n,) + v.shape)
    return lax.all_to_all(w, axis, 0, 0).sum(0)


def gather_points(v, x, y, c):
    def stage(v, shifts):
        return jnp.stack([v] + [lax.ppermute(v, "cent", cent_shift(*d)) for d in shifts])

    v = stage(v, [(0, k, 0) for k in (1, 2, 3)])
    v = stage(v, [(k, 0, 0) for k in (1, 2, 3)])
    v = stage(v, [(0, 0, 1)])
    xs = (x - jnp.arange(NX)) % NX
    ys = (y - jnp.arange(NY)) % NY
    cs = (c + jnp.arange(NC)) % NC
    v = v[cs][:, xs][:, :, ys]
    return v.transpose(1, 2, 0, 3, 4).reshape(NX * NY * NC * v.shape[3], v.shape[4])


def scatter_points(v, x, y, c):
    def pick(v, k, axis):
        return lax.dynamic_index_in_dim(v, k, axis, keepdims=False)

    rows, cols = v.shape
    v = v.reshape(NX, NY, NC, rows // (NX * NY * NC), cols)
    v = pick(v, c, 2) + lax.ppermute(pick(v, 1 - c, 2), "cent", cent_shift(0, 0, 1))
    v = sum(
        [lax.ppermute(pick(v, (x + k) % NX, 0), "cent", cent_shift(k, 0, 0)) for k in (1, 2, 3)],
        pick(v, x, 0),
    )
    v = sum(
        [lax.ppermute(pick(v, (y + k) % NY, 0), "cent", cent_shift(0, k, 0)) for k in (1, 2, 3)],
        pick(v, y, 0),
    )
    return v


def ring(part, z):
    half = part(0).shape[0] // 2
    first = part(z + 4)
    right = lax.ppermute(first[:half], "pts", z_shift(1))
    left = lax.ppermute(first[half:], "pts", z_shift(-1))
    for k in (3, 2, 1):
        a, b = part(z + k), part(z - k)
        if k == 3:
            a = jnp.concatenate([a[:half] + right, a[half:]])
            b = jnp.concatenate([b[:half], b[half:] + left])
        else:
            a, b = a + right, b + left
        right = lax.ppermute(a, "pts", z_shift(1))
        left = lax.ppermute(b, "pts", z_shift(-1))
    return part(z) + right + left


def split(v):
    hi = v.astype(jnp.bfloat16)
    lo = (v - hi.astype(jnp.float32)).astype(jnp.bfloat16)
    return hi, lo


def dot(a, b):
    return jnp.dot(a, b, preferred_element_type=jnp.float32)


def per_device(points, centroids):
    me = lax.axis_index("cent")
    z = lax.axis_index("pts")
    x, y, c = me // (NY * NC), (me // NC) % NY, me % NC
    zt = gather_points(points.T, x, y, c)
    rows = zt.shape[1]
    total = rows * NZ
    clusters = centroids.shape[0] * NX * NY * NC
    scale = 2.0 * clusters / total
    zf = zt.astype(jnp.float32)
    zsq = jnp.sum(zf * zf, axis=0)
    cf = centroids.astype(jnp.float32)
    msq = jnp.sum(cf * cf, axis=1)
    dots = dot(centroids, zt)
    kern = 1.0 / (1.0 + zsq[None, :] + msq[:, None] - 2.0 * dots)
    norm = sum_over(jnp.sum(kern, axis=0), "cent", 32)
    soft = kern / norm[None, :]
    freq = sum_over(jnp.sum(soft, axis=1), "pts", NZ)
    ratio = soft / freq[:, None]
    sharp = soft * ratio
    both = jnp.stack([jnp.sum(sharp, axis=0), jnp.sum(sharp * jnp.log(ratio * total), axis=0)])
    denom, cross = sum_over(both, "cent", 32)
    kl = jnp.sum(cross / denom - jnp.log(denom * total))
    loss = jnp.sum(sum_over(jnp.broadcast_to(kl, (128,)), "pts", NZ)[0]) / total
    coef = kern * (sharp / denom[None, :] - soft)
    hi, lo = split(coef)
    zn = zt.T
    g = dot(hi, zn) + dot(lo, zn) - jnp.sum(coef, axis=1)[:, None] * cf

    def part(owner):
        return lax.dynamic_slice_in_dim(g, (owner % NZ) * (g.shape[1] // NZ), g.shape[1] // NZ, axis=1)

    grad_centroids = -scale * ring(part, z)
    ct = centroids.T
    p = jnp.sum(coef, axis=0)[None, :] * zf - dot(ct, hi) - dot(ct, lo)
    grad_points = scale * scatter_points(p, x, y, c).T
    return (grad_points, grad_centroids, loss)


def solution(mesh):
    in_specs = (P("pts", "cent"), P("cent", None))
    out_specs = (P("pts", "cent"), P("cent", "pts"), P())
    return jax.shard_map(per_device, mesh=mesh, in_specs=in_specs, out_specs=out_specs, check_vma=False)
```

time: 453 us -> 278 us (0.61)
  blocking collectives: 217 us -> 31.1 us
  waiting for transfers between devices: 127 us -> 80.6 us
  starting transfers between devices: 0.34 us -> 43.8 us
  between operations: 15.6 us -> 2.55 us
  other arithmetic: 30.2 us -> 43.2 us
  local copies, waits for them, and re-layouts: 3.23 us -> 12.7 us
    psum x4 -> x0, blocking collectives: 217 us -> none  [the longest x1 76.3 us: per_device(): kl_sum = lax.psum(kl_part, ('pts', 'cent'))]
    reduce_scatter x2 -> x0, waiting for transfers between devices: 75.9 us -> none  [the longest x1 75.9 us: per_device(): part = lax.psum_scatter(term_cent, 'pts', scatter_dimension=1, tiled=True)]
    ppermute x0 -> x22, waiting for transfers between devices: none -> 63.6 us  [the longest x3 26.4 us: ring(): left = lax.ppermute(b, 'pts', z_shift(-1))]
    all_gather x1 -> x0, waiting for transfers between devices: 50.8 us -> none  [per_device(): zrows = lax.all_gather(points, 'cent', axis=1, tiled=True)]
    ppermute x0 -> x22, starting transfers between devices: none -> 35.5 us  [the longest x1 11 us: ring(): left = lax.ppermute(first[half:], 'pts', z_shift(-1))]
    all_to_all x0 -> x2, blocking collectives: none -> 31.1 us  [sum_over(): return lax.all_to_all(w, axis, 0, 0).sum(0)]
    all_to_all x0 -> x2, waiting for transfers between devices: none -> 17.1 us  [sum_over(): return lax.all_to_all(w, axis, 0, 0).sum(0)]
    add x1 -> x7, other arithmetic: 0.01 us -> 12 us  [the longest x3 7.5 us: ring(): a, b = (a + right, b + left)]
  transfers between devices with their start and end apart: 3 -> 24, of which waited for: 2 -> 15; matrix products, arithmetic and copies ran while one was open for 8% -> 16% of each run, Pallas kernels for 0% -> 0%
where the time goes in v1:
time: 278 us; the launch traced here: 274 us
  waiting for transfers between devices  80.6 us (29%)
  matrix products  59.9 us (22%)
  starting transfers between devices  43.8 us (16%)
  other arithmetic  43.2 us (16%)
  blocking collectives  31.1 us (11%)
  local copies, waits for them, and re-layouts  12.7 us (5%)
    dot_general x5, matrix products, dot(): return jnp.dot(a, b, preferred_element_type=jnp.float32)  59.9 us
    all_to_all x2, blocking collectives, sum_over(): return lax.all_to_all(w, axis, 0, 0).sum(0)  31.1 us
    ppermute x3, waiting for transfers between devices, ring(): left = lax.ppermute(b, 'pts', z_shift(-1))  26.4 us
    ppermute x3, waiting for transfers between devices, ring(): right = lax.ppermute(a, 'pts', z_shift(1))  21.1 us
    all_to_all x2, waiting for transfers between devices, sum_over(): return lax.all_to_all(w, axis, 0, 0).sum(0)  17.1 us
    ppermute x7, waiting for transfers between devices, stage(): lax.ppermute(v, 'cent', cent_shift(*d))  12.4 us
    ppermute x1, starting transfers between devices, ring(): left = lax.ppermute(first[half:], 'pts', z_shift(-1))  11 us
    ppermute x7, starting transfers between devices, stage(): lax.ppermute(v, 'cent', cent_shift(*d))  9.79 us
  transfers between devices with their start and end apart: 24, of which 15 were waited for; matrix products, arithmetic and copies ran while one was open for 16% of the time, Pallas kernels for 0%

profile of v1, /device:TPU:8, one launch (start us, length us, event | category | flops | bytes accessed | tf_op | source)
XLA Modules:
  0.0 273.9 jit_solution(13681339393849357800)
XLA Ops:
  0.6 2.4 collective-permute-start.1
  3.0 1.4 collective-permute-start
  5.0 1.7 collective-permute-done.1
  7.8 1.1 collective-permute-done.2
  9.7 2.1 collective-permute-start.4
  12.4 2.6 collective-permute-start.5
  15.0 5.5 %collective-permute-done.4 = bf16[4,32,1024]{2,1,0:T(8,128)(2,1)S(1)} collective-permute-done((bf16[4,32,1024]{2,1,0:T(8,128)(2,1)S(1)}, bf16[4,32,1024]{2,1,0:T(8,128)(2,1)S(1)}, u32[]{:S(2)}, u32[]{:S(2)}) %collective-permute-start.4) | collective-permute-done | bytes 262176 | tf_op jit(solution)/shard_map/ppermute | solution.py:35
  20.5 2.8 %collective-permute-done.3 = bf16[4,32,1024]{2,1,0:T(8,128)(2,1)S(1)} collective-permute-done((bf16[4,32,1024]{2,1,0:T(8,128)(2,1)S(1)}, bf16[4,32,1024]{2,1,0:T(8,128)(2,1)S(1)}, u32[]{:S(2)}, u32[]{:S(2)}) %collective-permute-start.3) | collective-permute-done | bytes 262176 | tf_op jit(solution)/shard_map/ppermute | solution.py:35
  24.0 3.1 %fusion = f32[2048]{0:T(1024)S(1)} fusion(bf16[2048,1024]{1,0:T(8,128)(2,1)} %param.3), kind=kLoop, calls=%fused_computation.5 | loop fusion | flops 6289408 | bytes 4202496 | tf_op jit(solution)/shard_map/reduce_sum | solution.py:104
  28.1 1.4 pad_maximum_fusion
  29.5 2.0 gather_fusion
  31.5 3.6 %gather_fusion.1 = bf16[4,2,4,32,1024]{4,3,2,1,0:T(8,128)(2,1)} fusion(bf16[2,4,4,32,1024]{4,3,2,1,0:T(8,128)(2,1)} %gather_fusion, s32[1024]{0:T(1024)S(1)} %pad_clamp_fusion.1), kind=kCustom, calls=%fused_computation.1 | custom fusion | bytes 4194320 | tf_op jit(solution)/shard_map/gather | solution.py:43
  35.1 2.3 gather_fusion.2
  38.0 11.0 %fusion.19 = (f32[1024]{0:T(1024)S(1)}, f32[1024,2048]{1,0:T(8,128)}) fusion(f32[2048]{0:T(1024)S(1)} %fusion, f32[1024]{0:T(1024)S(1)} %broadcast_add_fusion, bf16[1024,1024]{1,0:T(8,128)(2,1)S(1)} %bitcast.113, bf16[2048,1024]{1,0:T(8,128)(2,1)} %param.3), kind=kOutput, calls=%fused_computation.75 | convolution fusion | flops 4305452032 | bytes 14696448 | tf_op jit(solution)/shard_map/dot_general | solution.py:89
  49.2 14.5 %all_to_all.23 = f32[32,1,1024]{2,1,0:T(1,128)S(1)} all-to-all(f32[32,1,1024]{2,1,0:T(1,128)S(1)} %broadcast_in_dim.6), channel_id=1, replica_groups=mesh['pts'=8,'cent'=32] {'cent'}, dimensions={0} | all-to-all | bytes 262144 | tf_op jit(solution)/shard_map/all_to_all | solution.py:30
  63.7 4.4 %fusion.24 = f32[2048]{0:T(1024)S(1)} fusion(f32[1024]{0:T(1024)S(1)} %reduce_sum.120, f32[1024,2048]{1,0:T(8,128)} %get-tuple-element.29, f32[2048]{0:T(1024)S(1)} %fusion, f32[1024]{0:T(1024)S(1)} %broadcast_add_fusion), kind=kLoop, calls=%fused_computation.80 | loop fusion | flops 12580864 | bytes 8413184 | tf_op jit(solution)/shard_map/reduce_sum | solution.py:109
  68.2 16.7 %all_to_all.24 = f32[8,1,2048]{2,1,0:T(1,128)S(1)} all-to-all(f32[8,1,2048]{2,1,0:T(1,128)S(1)} %broadcast_in_dim.7), channel_id=1, replica_groups=mesh['pts'=8,'cent'=32] {'pts'}, dimensions={0} | all-to-all | bytes 131072 | tf_op jit(solution)/shard_map/all_to_all | solution.py:30
  84.9 6.9 %fusion.23 = (f32[1024]{0:T(1024)S(1)}, f32[1024]{0:T(1024)S(1)}) fusion(f32[2048]{0:T(1024)S(1)} %reduce_sum.122, f32[1024]{0:T(1024)S(1)} %reduce_sum.120, f32[1024,2048]{1,0:T(8,128)} %get-tuple-element.29, f32[2048]{0:T(1024)S(1)} %fusion, f32[1024]{0:T(1024)S(1)} %broadcast_add_fusion), kind=kLoop, calls=%fused_computation.79 | loop fusion | flops 25163776 | bytes 8421376 | tf_op jit(solution)/shard_map/reduce_sum | solution.py:112
  92.6 5.0 %all-to-all-start.2 = ((f32[32,2,1024]{2,1,0:T(2,128)}), f32[32,2,1024]{2,1,0:T(2,128)S(1)}, u32[]{:S(2)}, u32[]{:S(2)}) async-start(f32[32,2,1024]{2,1,0:T(2,128)} %broadcast_in_dim.8), calls=%async_computation.2 | async-start | bytes 524288 | tf_op jit(solution)/shard_map/all_to_all | solution.py:30
  97.7 7.4 %all-to-all-done.2 = f32[32,2,1024]{2,1,0:T(2,128)S(1)} async-done(((f32[32,2,1024]{2,1,0:T(2,128)}), f32[32,2,1024]{2,1,0:T(2,128)S(1)}, u32[]{:S(2)}, u32[]{:S(2)}) %all-to-all-start.2) | async-done | bytes 262176 | tf_op jit(solution)/shard_map/all_to_all | solution.py:30
  105.2 7.1 %fusion.25 = (f32[2048]{0:T(1024)S(1)}, f32[1024]{0:T(1024)S(1)}, f32[2048,1024]{0,1:T(8,128)S(1)}) fusion(f32[1024]{0:T(1024)S(1)} %bitcast.128, f32[2048]{0:T(1024)S(1)} %reduce_sum.122, f32[1024]{0:T(1024)S(1)} %reduce_sum.120, f32[1024,2048]{1,0:T(8,128)} %get-tuple-element.29, f32[2048]{0:T(1024)S(1)} %fusion, f32[1024]{0:T(1024)S(1)} %broadcast_add_fusion), kind=kLoop, calls=%fused_computation.81 | loop fusion | flops 29357056 | bytes 16818176 | tf_op jit(solution)/shard_map/reduce_sum | solution.py:119
  112.3 7.1 %fusion.15 = f32[2048,1024]{1,0:T(8,128)} fusion(bf16[1024,1024]{1,0:T(8,128)(2,1)S(1)} %bitcast.114, f32[2048,1024]{0,1:T(8,128)S(1)} %get-tuple-element.7), kind=kOutput, calls=%fused_computation.71 | convolution fusion | flops 4297064448 | bytes 18874368 | tf_op jit(solution)/shard_map/dot_general | solution.py:89
  119.3 18.6 %fusion.1 = f32[2048,1024]{1,0:T(8,128)S(1)} fusion(bf16[2048,1024]{1,0:T(8,128)(2,1)S(1)} %copy-done.3, f32[2048,1024]{1,0:T(8,128)} %fusion.15, f32[2048]{0:T(1024)S(1)} %get-tuple-element.5, bf16[1024,1024]{1,0:T(8,128)(2,1)S(1)} %bitcast.115, f32[2048,1024]{0,1:T(8,128)} %copy-done.1), kind=kOutput, calls=%fused_computation.6 | convolution fusion | flops 4311744512 | bytes 31465472 | tf_op jit(solution)/shard_map/dot_general | solution.py:89
  138.8 11.0 %collective-permute-start.18 = (f32[1024,128]{1,0:T(8,128)S(1)}, f32[1024,128]{1,0:T(8,128)S(1)}, u32[]{:S(2)}, u32[]{:S(2)}) collective-permute-start(f32[1024,128]{1,0:T(8,128)S(1)} %get-tuple-element.15), channel_id=1, source_target_pairs={{0,224},{32,0},{64,32},{96,64},{128,96},{160,128},{192,160},{224,1... | collective-permute-start | bytes 1572872 | tf_op jit(solution)/shard_map/ppermute | solution.py:69
  149.8 9.5 %fusion.17 = f32[1024,1024]{0,1:T(8,128)} fusion(bf16[2048,1024]{1,0:T(8,128)(2,1)S(1)} %copy-done.3, f32[2048,1024]{0,1:T(8,128)} %copy-done.1), kind=kOutput, calls=%fused_computation.73 | convolution fusion | flops 4297064448 | bytes 16777216 | tf_op jit(solution)/shard_map/dot_general | solution.py:89
  159.4 2.1 collective-permute-done.18
  163.3 13.6 %bitcast_subtract_fusion.1 = f32[1024,1024]{1,0:T(8,128)S(1)} fusion(f32[1024,1024]{0,1:T(8,128)} %fusion.17, bf16[1024,1024]{1,0:T(8,128)(2,1)S(1)} %bitcast.116, bf16[2048,1024]{1,0:T(8,128)(2,1)} %param.3, f32[1024]{0:T(1024)S(1)} %get-tuple-element.6, f32[2048,1024]{0,1:T(8,128)} %copy-done.1), kind=kOutput, calls=%fused_computation.14 | convolution fusion | flops 4307550208 | bytes 23072768 | tf_op jit(solution)/shard_map/dot_general | solution.py:89
  176.9 1.2 pad_maximum_fusion.3
  178.1 3.3 %collective-permute-start.19 = (f32[2048,128]{1,0:T(8,128)}, f32[2048,128]{1,0:T(8,128)}, u32[]{:S(2)}, u32[]{:S(2)}) collective-permute-start(f32[2048,128]{1,0:T(8,128)} %pad_maximum_fusion.3), channel_id=1, source_target_pairs={{0,224},{32,0},{64,32},{96,64},{128,96},{160,128},{192,160},{224,1... | collective-permute-start | bytes 3145736 | tf_op jit(solution)/shard_map/ppermute | solution.py:78
  181.4 8.4 %collective-permute-done.15 = f32[2048,128]{1,0:T(8,128)} collective-permute-done((f32[2048,128]{1,0:T(8,128)}, f32[2048,128]{1,0:T(8,128)}, u32[]{:S(2)}, u32[]{:S(2)}) %collective-permute-start.15) | collective-permute-done | bytes 1048608 | tf_op jit(solution)/shard_map/ppermute | solution.py:77
  189.7 1.4 dynamic-slice_add_fusion.2
  191.6 12.3 %collective-permute-done.19 = f32[2048,128]{1,0:T(8,128)} collective-permute-done((f32[2048,128]{1,0:T(8,128)}, f32[2048,128]{1,0:T(8,128)}, u32[]{:S(2)}, u32[]{:S(2)}) %collective-permute-start.19) | collective-permute-done | bytes 1048608 | tf_op jit(solution)/shard_map/ppermute | solution.py:78
  203.8 12.8 %collective-permute-done.16 = f32[2048,128]{1,0:T(8,128)} collective-permute-done((f32[2048,128]{1,0:T(8,128)S(1)}, f32[2048,128]{1,0:T(8,128)}, u32[]{:S(2)}, u32[]{:S(2)}) %collective-permute-start.16) | collective-permute-done | bytes 1048608 | tf_op jit(solution)/shard_map/ppermute | solution.py:77
  216.6 3.8 %dynamic-slice_add_fusion.3 = (f32[2048,128]{1,0:T(8,128)}, f32[2048,128]{1,0:T(8,128)}) fusion(f32[2048,128]{1,0:T(8,128)} %collective-permute-done.16, f32[2048,1024]{1,0:T(8,128)} %copy-done, s32[]{:T(128)S(6)} %select_n.227, f32[2048,128]{1,0:T(8,128)} %collective-permute-done.19, s32[]{:T(128)S(6)} %select_n.237), kind=kLoop, calls=%fused_computation.27 | loop fusion | flops 524288 | bytes 6291464 | tf_op jit(solution)/shard_map/add | solution.py:76
  220.7 2.6 bitcast_add_fusion
  223.4 1.2 dynamic-slice_bitcast_fusion.3
  225.6 2.2 collective-permute-start.10
  227.8 1.8 collective-permute-start.17
  229.6 14.2 %collective-permute-done.20 = f32[2048,128]{1,0:T(8,128)S(1)} collective-permute-done((f32[2048,128]{1,0:T(8,128)}, f32[2048,128]{1,0:T(8,128)S(1)}, u32[]{:S(2)}, u32[]{:S(2)}) %collective-permute-start.20) | collective-permute-done | bytes 1048608 | tf_op jit(solution)/shard_map/ppermute | solution.py:78
  243.8 2.3 dynamic-slice_add_fusion.1
  246.1 1.5 collective-permute-start.21
  249.1 1.5 fusion.4
  250.8 2.0 collective-permute-start.13
  252.8 1.1 collective-permute-start.12
  254.5 1.2 broadcast_in_dim_broadcast_in_dim_broadcast_in_dim.3
  255.8 3.3 %all-to-all-start.3 = ((f32[8,1,128]{2,1,0:T(1,128)}), f32[8,1,128]{2,1,0:T(1,128)S(1)}, u32[]{:S(2)}, u32[]{:S(2)}) async-start(f32[8,1,128]{2,1,0:T(1,128)} %broadcast_in_dim_broadcast_in_dim_broadcast_in_dim.3), calls=%async_computation.3 | async-start | bytes 8192 | tf_op jit(solution)/shard_map/all_to_all | solution.py:30
  259.1 9.7 %all-to-all-done.3 = f32[8,1,128]{2,1,0:T(1,128)S(1)} async-done(((f32[8,1,128]{2,1,0:T(1,128)}), f32[8,1,128]{2,1,0:T(1,128)S(1)}, u32[]{:S(2)}, u32[]{:S(2)}) %all-to-all-start.3) | async-done | bytes 4128 | tf_op jit(solution)/shard_map/all_to_all | solution.py:30
  269.6 3.0 %add_multiply_fusion = f32[2048,128]{1,0:T(8,128)} fusion(f32[2048,128]{1,0:T(8,128)} %collective-permute-done.21, f32[2048,128]{1,0:T(8,128)} %collective-permute-done.17, f32[2048,1024]{1,0:T(8,128)} %copy-done, s32[]{:T(128)S(6)} %select_n.225), kind=kLoop, calls=%fused_computation.23 | loop fusion | flops 786432 | bytes 4194308 | tf_op jit(solution)/shard_map/mul | solution.py:124
  (65 shorter events, 13.9 us)
Async XLA Ops:
  0.6 6.1 %collective-permute-start.1 = (bf16[32,1024]{1,0:T(8,128)(2,1)}, bf16[32,1024]{1,0:T(8,128)(2,1)S(1)}, u32[]{:S(2)}, u32[]{:S(2)}) collective-permute-start(bf16[32,1024]{1,0:T(8,128)(2,1)} %bitcast.121), channel_id=1, source_target_pairs={{0,4},{1,5},{2,6},{3,7},{4,0},{5,1},{6,2},{7,3},{8,12},{9,13},{10,... | collective-permute-start | bytes 196616 | tf_op jit(solution)/shard_map/ppermute | solution.py:35
  3.0 4.8 %collective-permute-start = (bf16[32,1024]{1,0:T(8,128)(2,1)}, bf16[32,1024]{1,0:T(8,128)(2,1)S(1)}, u32[]{:S(2)}, u32[]{:S(2)}) collective-permute-start(bf16[32,1024]{1,0:T(8,128)(2,1)} %bitcast.122), channel_id=1, source_target_pairs={{0,2},{1,3},{2,4},{3,5},{4,6},{5,7},{6,0},{7,1},{8,10},{9,11},{10,... | collective-permute-start | bytes 196616 | tf_op jit(solution)/shard_map/ppermute | solution.py:35
  4.4 4.5 %collective-permute-start.2 = (bf16[32,1024]{1,0:T(8,128)(2,1)}, bf16[32,1024]{1,0:T(8,128)(2,1)S(1)}, u32[]{:S(2)}, u32[]{:S(2)}) collective-permute-start(bf16[32,1024]{1,0:T(8,128)(2,1)} %bitcast.123), channel_id=1, source_target_pairs={{0,6},{1,7},{2,0},{3,1},{4,2},{5,3},{6,4},{7,5},{8,14},{9,15},{10,... | collective-permute-start | bytes 196616 | tf_op jit(solution)/shard_map/ppermute | solution.py:35
  9.7 10.8 %collective-permute-start.4 = (bf16[4,32,1024]{2,1,0:T(8,128)(2,1)S(1)}, bf16[4,32,1024]{2,1,0:T(8,128)(2,1)S(1)}, u32[]{:S(2)}, u32[]{:S(2)}) collective-permute-start(bf16[4,32,1024]{2,1,0:T(8,128)(2,1)S(1)} %get-tuple-element.25), channel_id=1, source_target_pairs={{0,16},{1,17},{2,18},{3,19},{4,20},{5,21},{6,22},{7,23},{8,24},{9,... | collective-permute-start | bytes 786440 | tf_op jit(solution)/shard_map/ppermute | solution.py:35
  11.8 11.5 %collective-permute-start.3 = (bf16[4,32,1024]{2,1,0:T(8,128)(2,1)S(1)}, bf16[4,32,1024]{2,1,0:T(8,128)(2,1)S(1)}, u32[]{:S(2)}, u32[]{:S(2)}) collective-permute-start(bf16[4,32,1024]{2,1,0:T(8,128)(2,1)S(1)} %get-tuple-element.25), channel_id=1, source_target_pairs={{0,8},{1,9},{2,10},{3,11},{4,12},{5,13},{6,14},{7,15},{8,16},{9,17... | collective-permute-start | bytes 786440 | tf_op jit(solution)/shard_map/ppermute | solution.py:35
  12.4 11.2 %collective-permute-start.5 = (bf16[4,32,1024]{2,1,0:T(8,128)(2,1)S(1)}, bf16[4,32,1024]{2,1,0:T(8,128)(2,1)S(1)}, u32[]{:S(2)}, u32[]{:S(2)}) collective-permute-start(bf16[4,32,1024]{2,1,0:T(8,128)(2,1)S(1)} %get-tuple-element.25), channel_id=1, source_target_pairs={{0,24},{1,25},{2,26},{3,27},{4,28},{5,29},{6,30},{7,31},{8,0},{9,1... | collective-permute-start | bytes 786440 | tf_op jit(solution)/shard_map/ppermute | solution.py:35
  23.8 3.3 %collective-permute-start.6 = (bf16[4,4,32,1024]{3,2,1,0:T(8,128)(2,1)S(1)}, bf16[4,4,32,1024]{3,2,1,0:T(8,128)(2,1)S(1)}, u32[]{:S(2)}, u32[]{:S(2)}) collective-permute-start(bf16[4,4,32,1024]{3,2,1,0:T(8,128)(2,1)S(1)} %get-tuple-element.20), channel_id=1, source_target_pairs={{0,1},{1,0},{2,3},{3,2},{4,5},{5,4},{6,7},{7,6},{8,9},{9,8},{10,11... | collective-permute-start | bytes 3145736 | tf_op jit(solution)/shard_map/ppermute | solution.py:35
  27.1 1.0 copy-start.6
  38.0 11.1 %copy-start.4 = (bf16[4,4,2,32,1024]{4,3,2,1,0:T(8,128)(2,1)}, bf16[4,4,2,32,1024]{4,3,2,1,0:T(8,128)(2,1)S(1)}, u32[]{:S(2)}) copy-start(bf16[4,4,2,32,1024]{4,3,2,1,0:T(8,128)(2,1)S(1)} %copy.7) | copy-start | bytes 6291460
  92.6 12.5 %all-to-all-start.2 = ((f32[32,2,1024]{2,1,0:T(2,128)}), f32[32,2,1024]{2,1,0:T(2,128)S(1)}, u32[]{:S(2)}, u32[]{:S(2)}) async-start(f32[32,2,1024]{2,1,0:T(2,128)} %broadcast_in_dim.8), calls=%async_computation.2 | async-start | bytes 524288 | tf_op jit(solution)/shard_map/all_to_all | solution.py:30
  105.2 7.1 %copy-start.5 = (bf16[4,4,2,32,1024]{4,3,2,1,0:T(8,128)(2,1)S(1)}, bf16[4,4,2,32,1024]{4,3,2,1,0:T(8,128)(2,1)}, u32[]{:S(2)}) copy-start(bf16[4,4,2,32,1024]{4,3,2,1,0:T(8,128)(2,1)} %copy-done.4) | copy-start | bytes 6291460
  112.2 7.1 %copy-start.1 = (f32[2048,1024]{0,1:T(8,128)}, f32[2048,1024]{0,1:T(8,128)S(1)}, u32[]{:S(2)}) copy-start(f32[2048,1024]{0,1:T(8,128)S(1)} %get-tuple-element.7) | copy-start | bytes 25165828
  112.3 7.1 %copy-start.3 = (bf16[2048,1024]{1,0:T(8,128)(2,1)S(1)}, bf16[2048,1024]{1,0:T(8,128)(2,1)}, u32[]{:S(2)}) copy-start(bf16[2048,1024]{1,0:T(8,128)(2,1)} %param.3) | copy-start | bytes 12582916
  138.0 51.8 %copy-start = (f32[2048,1024]{1,0:T(8,128)}, f32[2048,1024]{1,0:T(8,128)S(1)}, u32[]{:S(2)}) copy-start(f32[2048,1024]{1,0:T(8,128)S(1)} %fusion.1) | copy-start | bytes 25165828
  138.2 21.2 %collective-permute-start.14 = (f32[1024,128]{1,0:T(8,128)S(1)}, f32[1024,128]{1,0:T(8,128)S(1)}, u32[]{:S(2)}, u32[]{:S(2)}) collective-permute-start(f32[1024,128]{1,0:T(8,128)S(1)} %get-tuple-element.14), channel_id=1, source_target_pairs={{0,32},{32,64},{64,96},{96,128},{128,160},{160,192},{192,224},{224... | collective-permute-start | bytes 1572872 | tf_op jit(solution)/shard_map/ppermute | solution.py:68
  138.8 22.7 %collective-permute-start.18 = (f32[1024,128]{1,0:T(8,128)S(1)}, f32[1024,128]{1,0:T(8,128)S(1)}, u32[]{:S(2)}, u32[]{:S(2)}) collective-permute-start(f32[1024,128]{1,0:T(8,128)S(1)} %get-tuple-element.15), channel_id=1, source_target_pairs={{0,224},{32,0},{64,32},{96,64},{128,96},{160,128},{192,160},{224,1... | collective-permute-start | bytes 1572872 | tf_op jit(solution)/shard_map/ppermute | solution.py:69
  162.9 26.9 %collective-permute-start.15 = (f32[2048,128]{1,0:T(8,128)}, f32[2048,128]{1,0:T(8,128)}, u32[]{:S(2)}, u32[]{:S(2)}) collective-permute-start(f32[2048,128]{1,0:T(8,128)} %pad_maximum_fusion.2), channel_id=1, source_target_pairs={{0,32},{32,64},{64,96},{96,128},{128,160},{160,192},{192,224},{224... | collective-permute-start | bytes 3145736 | tf_op jit(solution)/shard_map/ppermute | solution.py:77
  176.9 14.3 %copy-start.2 = (f32[1024,1024]{1,0:T(8,128)}, f32[1024,1024]{1,0:T(8,128)S(1)}, u32[]{:S(2)}) copy-start(f32[1024,1024]{1,0:T(8,128)S(1)} %bitcast_subtract_fusion.1) | copy-start | bytes 12582916
  178.1 25.7 %collective-permute-start.19 = (f32[2048,128]{1,0:T(8,128)}, f32[2048,128]{1,0:T(8,128)}, u32[]{:S(2)}, u32[]{:S(2)}) collective-permute-start(f32[2048,128]{1,0:T(8,128)} %pad_maximum_fusion.3), channel_id=1, source_target_pairs={{0,224},{32,0},{64,32},{96,64},{128,96},{160,128},{192,160},{224,1... | collective-permute-start | bytes 3145736 | tf_op jit(solution)/shard_map/ppermute | solution.py:78
  191.2 25.4 %collective-permute-start.16 = (f32[2048,128]{1,0:T(8,128)S(1)}, f32[2048,128]{1,0:T(8,128)}, u32[]{:S(2)}, u32[]{:S(2)}) collective-permute-start(f32[2048,128]{1,0:T(8,128)S(1)} %dynamic-slice_add_fusion.2), channel_id=1, source_target_pairs={{0,32},{32,64},{64,96},{96,128},{128,160},{160,192},{192,224},{224... | collective-permute-start | bytes 3145736 | tf_op jit(solution)/shard_map/ppermute | solution.py:77
  191.4 29.3 %collective-permute-start.7 = (f32[4,4,32,1024]{3,2,1,0:T(8,128)S(1)}, f32[4,4,32,1024]{3,2,1,0:T(8,128)}, u32[]{:S(2)}, u32[]{:S(2)}) collective-permute-start(f32[4,4,32,1024]{3,2,1,0:T(8,128)S(1)} %dynamic-slice_bitcast_fusion), channel_id=1, source_target_pairs={{0,1},{1,0},{2,3},{3,2},{4,5},{5,4},{6,7},{7,6},{8,9},{9,8},{10,11... | collective-permute-start | bytes 6291464 | tf_op jit(solution)/shard_map/ppermute | solution.py:53
  220.3 23.5 %collective-permute-start.20 = (f32[2048,128]{1,0:T(8,128)}, f32[2048,128]{1,0:T(8,128)S(1)}, u32[]{:S(2)}, u32[]{:S(2)}) collective-permute-start(f32[2048,128]{1,0:T(8,128)} %get-tuple-element.9), channel_id=1, source_target_pairs={{0,224},{32,0},{64,32},{96,64},{128,96},{160,128},{192,160},{224,1... | collective-permute-start | bytes 3145736 | tf_op jit(solution)/shard_map/ppermute | solution.py:78
  224.6 23.1 %collective-permute-start.8 = (f32[4,32,1024]{2,1,0:T(8,128)}, f32[4,32,1024]{2,1,0:T(8,128)}, u32[]{:S(2)}, u32[]{:S(2)}) collective-permute-start(f32[4,32,1024]{2,1,0:T(8,128)} %get-tuple-element.16), channel_id=1, source_target_pairs={{0,8},{1,9},{2,10},{3,11},{4,12},{5,13},{6,14},{7,15},{8,16},{9,17... | collective-permute-start | bytes 1572872 | tf_op jit(solution)/shard_map/ppermute | solution.py:55
  225.6 22.8 %collective-permute-start.10 = (f32[4,32,1024]{2,1,0:T(8,128)}, f32[4,32,1024]{2,1,0:T(8,128)}, u32[]{:S(2)}, u32[]{:S(2)}) collective-permute-start(f32[4,32,1024]{2,1,0:T(8,128)} %get-tuple-element.17), channel_id=1, source_target_pairs={{0,24},{1,25},{2,26},{3,27},{4,28},{5,29},{6,30},{7,31},{8,0},{9,1... | collective-permute-start | bytes 1572872 | tf_op jit(solution)/shard_map/ppermute | solution.py:55
  227.8 21.3 %collective-permute-start.9 = (f32[4,32,1024]{2,1,0:T(8,128)}, f32[4,32,1024]{2,1,0:T(8,128)}, u32[]{:S(2)}, u32[]{:S(2)}) collective-permute-start(f32[4,32,1024]{2,1,0:T(8,128)} %get-tuple-element.18), channel_id=1, source_target_pairs={{0,16},{1,17},{2,18},{3,19},{4,20},{5,21},{6,22},{7,23},{8,24},{9,... | collective-permute-start | bytes 1572872 | tf_op jit(solution)/shard_map/ppermute | solution.py:55
  227.8 41.8 %collective-permute-start.17 = (f32[2048,128]{1,0:T(8,128)}, f32[2048,128]{1,0:T(8,128)}, u32[]{:S(2)}, u32[]{:S(2)}) collective-permute-start(f32[2048,128]{1,0:T(8,128)} %get-tuple-element.8), channel_id=1, source_target_pairs={{0,32},{32,64},{64,96},{96,128},{128,160},{160,192},{192,224},{224... | collective-permute-start | bytes 3145736 | tf_op jit(solution)/shard_map/ppermute | solution.py:77
  246.1 23.4 %collective-permute-start.21 = (f32[2048,128]{1,0:T(8,128)}, f32[2048,128]{1,0:T(8,128)}, u32[]{:S(2)}, u32[]{:S(2)}) collective-permute-start(f32[2048,128]{1,0:T(8,128)} %dynamic-slice_add_fusion.1), channel_id=1, source_target_pairs={{0,224},{32,0},{64,32},{96,64},{128,96},{160,128},{192,160},{224,1... | collective-permute-start | bytes 3145736 | tf_op jit(solution)/shard_map/ppermute | solution.py:78
  250.7 18.2 %collective-permute-start.11 = (f32[32,1024]{1,0:T(8,128)S(1)}, f32[32,1024]{1,0:T(8,128)S(1)}, u32[]{:S(2)}, u32[]{:S(2)}) collective-permute-start(f32[32,1024]{1,0:T(8,128)S(1)} %get-tuple-element.21), channel_id=1, source_target_pairs={{0,2},{1,3},{2,4},{3,5},{4,6},{5,7},{6,0},{7,1},{8,10},{9,11},{10,... | collective-permute-start | bytes 393224 | tf_op jit(solution)/shard_map/ppermute | solution.py:59
  250.8 18.1 %collective-permute-start.13 = (f32[32,1024]{1,0:T(8,128)S(1)}, f32[32,1024]{1,0:T(8,128)S(1)}, u32[]{:S(2)}, u32[]{:S(2)}) collective-permute-start(f32[32,1024]{1,0:T(8,128)S(1)} %get-tuple-element.22), channel_id=1, source_target_pairs={{0,6},{1,7},{2,0},{3,1},{4,2},{5,3},{6,4},{7,5},{8,14},{9,15},{10,... | collective-permute-start | bytes 393224 | tf_op jit(solution)/shard_map/ppermute | solution.py:59
  252.8 16.1 %collective-permute-start.12 = (f32[32,1024]{1,0:T(8,128)S(1)}, f32[32,1024]{1,0:T(8,128)S(1)}, u32[]{:S(2)}, u32[]{:S(2)}) collective-permute-start(f32[32,1024]{1,0:T(8,128)S(1)} %get-tuple-element.23), channel_id=1, source_target_pairs={{0,4},{1,5},{2,6},{3,7},{4,0},{5,1},{6,2},{7,3},{8,12},{9,13},{10,... | collective-permute-start | bytes 393224 | tf_op jit(solution)/shard_map/ppermute | solution.py:59
  255.8 13.0 %all-to-all-start.3 = ((f32[8,1,128]{2,1,0:T(1,128)}), f32[8,1,128]{2,1,0:T(1,128)S(1)}, u32[]{:S(2)}, u32[]{:S(2)}) async-start(f32[8,1,128]{2,1,0:T(1,128)} %broadcast_in_dim_broadcast_in_dim_broadcast_in_dim.3), calls=%async_computation.3 | async-start | bytes 8192 | tf_op jit(solution)/shard_map/all_to_all | solution.py:30

commit v2 on v0

v2 whole, which is shorter than its diff:
```python
import functools

import jax
import jax.numpy as jnp
from jax import lax
from jax.experimental import pallas as pl
from jax.experimental.pallas import tpu as pltpu
from jax.sharding import PartitionSpec as P

NX, NY, NC, NZ = 4, 4, 2, 8
NCENT = NX * NY * NC
D = 1024
ROWS = 1024
CENT = 2048
TOTAL = ROWS * NZ
SCALE = 2.0 * CENT * NCENT / TOTAL
CHUNK = D // NZ
HALF = CENT // 2
PAD = 16
TILE = 256
STEPS = CENT // TILE
WIDE = 512
SLAB = 256
WSTEPS = CENT // WIDE
BLOCK = D // NCENT
LANES = 128
F32 = jnp.float32
BF16 = jnp.bfloat16
POWER, WIDTH, SHIFT = 31.0, 255.0, 125.0


def cent_id(x, y, c):
    return (x * NY + y) * NC + c


def cent_shift(dx, dy, dc):
    pairs = []
    for x in range(NX):
        for y in range(NY):
            for c in range(NC):
                pairs.append((cent_id(x, y, c), cent_id((x + dx) % NX, (y + dy) % NY, c ^ dc)))
    return pairs


def z_shift(k):
    return [(i, (i + k) % NZ) for i in range(NZ)]


def dot(a, b):
    return jnp.dot(a, b, preferred_element_type=F32)


def as_row(tile):
    return jnp.concatenate([tile[k : k + 1, :] for k in range(tile.shape[0])], axis=1)


def store_tile(ref, row, lead, first):
    for k in range(row.shape[1] // LANES):
        piece = row[:, k * LANES : (k + 1) * LANES]
        ref[:, first + k, :] = jnp.broadcast_to(piece, (lead, LANES))


def column_blocks(tile, first, count):
    cols = []
    for k in range(count):
        row = tile[first + k : first + k + 1, :]
        cols.append(jnp.transpose(jnp.broadcast_to(row, (LANES, LANES))))
    return jnp.concatenate(cols, axis=0)


def lane_wide(col, width):
    return jnp.concatenate([col] * (width // LANES), axis=1)


def lane_fold(v):
    return functools.reduce(jnp.add, [v[:, k * LANES : (k + 1) * LANES] for k in range(v.shape[1] // LANES)])


def call(body, grid, in_specs, out_specs, out_shape, scratch=(), prefetch=0, vmem=8, flops=0, nbytes=0):
    return pl.pallas_call(
        body,
        grid_spec=pltpu.PrefetchScalarGridSpec(
            num_scalar_prefetch=prefetch,
            grid=grid,
            in_specs=in_specs,
            out_specs=out_specs,
            scratch_shapes=list(scratch),
        ),
        out_shape=out_shape,
        compiler_params=pltpu.CompilerParams(
            dimension_semantics=("arbitrary",) * len(grid), vmem_limit_bytes=vmem << 20
        ),
        cost_estimate=pl.CostEstimate(flops=flops, bytes_accessed=nbytes, transcendentals=0),
    )


def in_hbm(v):
    return pltpu.with_memory_space_constraint(v, pltpu.HBM)


def whole(shape):
    return pl.BlockSpec(shape, lambda *_: (0,) * len(shape))


def shaped(shape, dtype=F32):
    return jax.ShapeDtypeStruct(shape, dtype)


def kern_body(at, mine, other, cent, kern, norm, zt, zn, zsq, acc, sems):
    step = pl.program_id(0)

    @pl.when(step == 0)
    def _():
        copies = []
        for cr in range(NC):
            src = (mine, other)[cr]
            for xr in range(NX):
                for yr in range(NY):
                    xx = lax.rem(at[0] + NX - xr, NX)
                    yy = lax.rem(at[1] + NY - yr, NY)
                    cc = lax.rem(at[2] + cr, NC)
                    row = pl.multiple_of(((xx * NY + yy) * NC + cc) * BLOCK, BLOCK)
                    copies.append(
                        pltpu.make_async_copy(
                            src.at[xr, yr], zt.at[pl.ds(row, BLOCK), :], sems.at[(cr * NX + xr) * NY + yr]
                        )
                    )
        for cp in copies:
            cp.start()
        for cp in copies:
            cp.wait()
        total = jnp.zeros((8, ROWS), F32)
        for k in range(D // LANES):
            v = zt[k * LANES : (k + 1) * LANES, :].astype(F32)
            v = v * v
            total = total + jnp.sum(v.reshape(LANES // 8, 8, ROWS), axis=0)
        zsq[...] = 1.0 + jnp.sum(total, axis=0, keepdims=True)
        acc[...] = jnp.zeros_like(acc)

    c = cent[...]
    cf = c.astype(F32)
    msq = jnp.sum(lane_fold(cf * cf), axis=1, keepdims=True)
    for k in range(ROWS // SLAB):
        cols = slice(k * SLAB, (k + 1) * SLAB)
        dots = dot(c, zt[:, cols])
        v = 1.0 / ((zsq[:, cols] + msq) - 2.0 * dots)
        kern[:, cols] = v
        acc[:, cols] += jnp.sum(v.reshape(WIDE // 8, 8, SLAB), axis=0)
    part = D // WSTEPS
    first = pl.multiple_of(step * part, part)
    zn[:, pl.ds(first, part)] = jnp.transpose(zt[pl.ds(first, part), :])

    @pl.when(step == WSTEPS - 1)
    def _():
        store_tile(norm, jnp.sum(acc[...], axis=0, keepdims=True), NCENT, 0)


def kern_call(at, mine, other, centroids):
    return call(
        kern_body,
        (WSTEPS,),
        [
            pl.BlockSpec(memory_space=pl.ANY),
            pl.BlockSpec(memory_space=pl.ANY),
            pl.BlockSpec((WIDE, D), lambda s, *_: (s, 0)),
        ],
        [
            pl.BlockSpec((WIDE, ROWS), lambda s, *_: (s, 0)),
            whole((NCENT, 8, LANES)),
            whole((D, ROWS)),
            whole((ROWS, D)),
        ],
        [shaped((CENT, ROWS)), shaped((NCENT, 8, LANES)), shaped((D, ROWS), BF16), shaped((ROWS, D), BF16)],
        [pltpu.VMEM((1, ROWS), F32), pltpu.VMEM((8, ROWS), F32), pltpu.SemaphoreType.DMA((NCENT,))],
        prefetch=1,
        vmem=14,
        flops=2 * CENT * ROWS * D,
        nbytes=20 << 20,
    )(at, mine, other, in_hbm(centroids))


def freq_body(norms, kern, freq, inv, row):
    step = pl.program_id(0)

    @pl.when(step == 0)
    def _():
        tile = 1.0 / jnp.sum(norms[...], axis=0)
        inv[...] = tile
        row[...] = as_row(tile)

    part = lane_fold(kern[...] * row[...])
    for k in range(TILE // LANES):
        block = jnp.transpose(part[k * LANES : (k + 1) * LANES, :])
        line = jnp.sum(block, axis=0, keepdims=True)
        freq[:, pl.ds(step * (TILE // LANES) + k, 1), :] = jnp.broadcast_to(line[None], (NZ, 1, LANES))


def freq_call(norms, kern):
    return call(
        freq_body,
        (STEPS,),
        [whole((NCENT, 8, LANES)), pl.BlockSpec((TILE, ROWS), lambda s: (s, 0))],
        [whole((NZ, CENT // LANES, LANES)), whole((8, LANES))],
        [shaped((NZ, CENT // LANES, LANES)), shaped((8, LANES))],
        [pltpu.VMEM((1, ROWS), F32)],
        vmem=6,
        flops=CENT * ROWS * 2,
        nbytes=8 << 20,
    )(norms, kern)


def frequency_columns(rf, step):
    tile = rf[pl.ds(pl.multiple_of(step * (TILE // LANES), TILE // LANES), TILE // LANES), :]
    return lane_wide(column_blocks(tile, 0, TILE // LANES), ROWS)


def denom_body(freqs, inv, kern, out, rf, row, dsum, csum):
    step = pl.program_id(0)

    @pl.when(step == 0)
    def _():
        rf[...] = 1.0 / jnp.sum(freqs[...], axis=0)
        row[...] = as_row(inv[...])
        dsum[...] = jnp.zeros_like(dsum)
        csum[...] = jnp.zeros_like(csum)

    soft = kern[...] * row[...]
    ratio = soft * frequency_columns(rf, step)
    sharp = soft * ratio
    dsum[...] += jnp.sum(sharp.reshape(TILE // 8, 8, ROWS), axis=0)
    csum[...] += jnp.sum((sharp * jnp.log(ratio * float(TOTAL))).reshape(TILE // 8, 8, ROWS), axis=0)

    @pl.when(step == STEPS - 1)
    def _():
        store_tile(out, jnp.sum(dsum[...], axis=0, keepdims=True), NCENT, 0)
        store_tile(out, jnp.sum(csum[...], axis=0, keepdims=True), NCENT, 8)


def denom_call(freqs, inv, kern):
    return call(
        denom_body,
        (STEPS,),
        [
            whole((NZ, CENT // LANES, LANES)),
            whole((8, LANES)),
            pl.BlockSpec((TILE, ROWS), lambda s: (s, 0)),
        ],
        whole((NCENT, 16, LANES)),
        shaped((NCENT, 16, LANES)),
        [
            pltpu.VMEM((CENT // LANES, LANES), F32),
            pltpu.VMEM((1, ROWS), F32),
            pltpu.VMEM((8, ROWS), F32),
            pltpu.VMEM((8, ROWS), F32),
        ],
        vmem=8,
        flops=CENT * ROWS * 6,
        nbytes=8 << 20,
    )(freqs, inv, kern)


def exponent(v):
    size = jnp.abs(v)
    top = jnp.maximum(jnp.max(jnp.max(size, axis=0, keepdims=True), axis=1, keepdims=True), 1e-30)
    return jnp.ceil(jnp.log2(top))


def code(v, expo):
    unit = jnp.minimum(jnp.abs(v) * jnp.exp2(-expo), 1.0)
    c = jnp.exp2(POWER * jnp.log2(1.0 + WIDTH * unit) - SHIFT)
    return jnp.where(v < 0.0, -c, c).astype(BF16)


def uncode(c, expo):
    c = c.astype(F32)
    unit = (jnp.exp2((jnp.log2(jnp.abs(c)) + SHIFT) * (1.0 / POWER)) - 1.0) * (1.0 / WIDTH)
    unit = unit * jnp.exp2(expo)
    return jnp.where(c < 0.0, -unit, unit)


def encode(v, slots, msg):
    rows = v.shape[0]
    expo = exponent(v)
    msg[:rows, :] = code(v, expo)
    high = slots.astype(BF16).astype(F32)
    mid = (slots - high).astype(BF16).astype(F32)
    low = slots - high - mid
    tail = [jnp.broadcast_to(expo, (1, v.shape[1])), high, mid, low, jnp.zeros((PAD - 4, v.shape[1]), F32)]
    msg[rows:, :] = jnp.concatenate(tail, axis=0).astype(BF16)


def decode(msg):
    rows = msg.shape[0] - PAD
    tail = msg[rows:, :].astype(F32)
    return uncode(msg[:rows, :], tail[0:1, :]), (tail[1:2, :] + tail[2:3, :]) + tail[3:4, :]


MSG = (CENT + PAD, CHUNK)
FIRST = (HALF + PAD, CHUNK)


def coef_body(z, dens, freqs, inv, kern, cent, zn, hi, lo, csum, kl, g, right, left, rf, row, rden, first):
    step = pl.program_id(0)

    @pl.when(step == 0)
    def _():
        rf[...] = 1.0 / jnp.sum(freqs[...], axis=0)
        row[...] = as_row(inv[...])
        both = jnp.sum(dens[...], axis=0)
        rtile = 1.0 / both[:8]
        rden[...] = as_row(rtile)
        part = both[8:] * rtile - jnp.log(both[:8] * float(TOTAL))
        part = jnp.sum(jnp.sum(part, axis=0, keepdims=True), axis=1, keepdims=True) * (1.0 / TOTAL)
        lane = lax.broadcasted_iota(jnp.int32, kl.shape, 1)
        kl[...] = jnp.where(lane == z[0], jnp.broadcast_to(part, kl.shape), 0.0)
        csum[...] = jnp.zeros_like(csum)

    far = lax.rem(z[0] + NZ // 2, NZ)
    total = jnp.zeros((8, ROWS), F32)
    for sub in range(WIDE // TILE):
        at = slice(sub * TILE, (sub + 1) * TILE)
        k = kern[at, :]
        soft = k * row[...]
        fc = frequency_columns(rf, step * (WIDE // TILE) + sub)
        coef = k * (soft * soft * fc * rden[...] - soft)
        h = coef.astype(BF16)
        l = (coef - h.astype(F32)).astype(BF16)
        hi[at, :] = h
        lo[at, :] = l
        total = total + jnp.sum(coef.reshape(TILE // 8, 8, ROWS), axis=0)
        e = jnp.sum(lane_fold(coef), axis=1, keepdims=True)
        both = jnp.concatenate([h, l], axis=0)
        for n in range(D // SLAB):
            cols = slice(n * SLAB, (n + 1) * SLAB)
            r = dot(both, zn[:, cols])
            r = r[:TILE] + r[TILE:] - e * cent[at, cols].astype(F32)
            for o in range(SLAB // CHUNK):
                g[n * (SLAB // CHUNK) + o, at, :] = r[:, o * CHUNK : (o + 1) * CHUNK]
    csum[...] += total
    first[pl.ds(pl.multiple_of(step * WIDE, WIDE), WIDE), :] = g[pl.ds(far, 1)][0]

    @pl.when(step == WSTEPS - 1)
    def _():
        encode(first[:HALF, :], kl[0:1, :], right)
        encode(first[HALF:, :], jnp.zeros((1, LANES), F32), left)


def coef_call(z, dens, freqs, inv, kern, centroids, zn):
    tiles = pl.BlockSpec((WIDE, ROWS), lambda s, z: (s, 0))
    return call(
        coef_body,
        (WSTEPS,),
        [
            whole((NCENT, 16, LANES)),
            whole((NZ, CENT // LANES, LANES)),
            whole((8, LANES)),
            tiles,
            pl.BlockSpec((WIDE, D), lambda s, z: (s, 0)),
            whole((ROWS, D)),
        ],
        [
            tiles,
            tiles,
            whole((8, ROWS)),
            whole((8, LANES)),
            pl.BlockSpec((NZ, WIDE, CHUNK), lambda s, z: (0, s, 0)),
            whole(FIRST),
            whole(FIRST),
        ],
        [
            shaped((CENT, ROWS), BF16),
            shaped((CENT, ROWS), BF16),
            shaped((8, ROWS)),
            shaped((8, LANES)),
            shaped((NZ, CENT, CHUNK)),
            shaped(FIRST, BF16),
            shaped(FIRST, BF16),
        ],
        [
            pltpu.VMEM((CENT // LANES, LANES), F32),
            pltpu.VMEM((1, ROWS), F32),
            pltpu.VMEM((1, ROWS), F32),
            pltpu.VMEM((CENT, CHUNK), F32),
        ],
        prefetch=1,
        vmem=18,
        flops=4 * CENT * ROWS * D,
        nbytes=30 << 20,
    )(z, dens, freqs, inv, kern, in_hbm(centroids), zn)


def hop_body(k, at, a, b, kl, got_right, got_left, right, left):
    for part, got, msg, first in ((a, got_right, right, 0), (b, got_left, left, HALF)):
        v, slots = decode(got)
        full = part[0]
        if k == NZ // 2 - 1:
            own = full[first : first + HALF, :] + v
            rest = full[HALF - first : CENT - first, :]
            full = jnp.concatenate([own, rest] if first == 0 else [rest, own], axis=0)
        else:
            full = full + v
        encode(full, slots + kl[0:1, :], msg)


def part_spec(k):
    return pl.BlockSpec((1, CENT, CHUNK), lambda s, z: (lax.rem(z[0] + k + NZ, NZ), 0, 0))


def hop_call(z, g, kl, k, got):
    return call(
        functools.partial(hop_body, k),
        (1,),
        [part_spec(k), part_spec(-k), whole((8, LANES)), whole(got[0].shape), whole(got[1].shape)],
        [whole(MSG), whole(MSG)],
        [shaped(MSG, BF16)] * 2,
        prefetch=1,
        vmem=14,
        flops=4 * CENT * CHUNK * 40,
        nbytes=3 << 20,
    )(z, g, g, kl, *got)


def end_body(at, own, kl, right, left, out, loss):
    (r, before), (l, after) = decode(right), decode(left)
    out[...] = (own[0] + r + l) * -SCALE
    total = jnp.sum(kl[0:1, :] + before + after, axis=1, keepdims=True)
    loss[...] = jnp.broadcast_to(total, loss.shape)


def end_call(z, g, kl, right, left):
    return call(
        end_body,
        (1,),
        [part_spec(0), whole((8, LANES)), whole(MSG), whole(MSG)],
        [whole((CENT, CHUNK)), whole((8, LANES))],
        [shaped((CENT, CHUNK)), shaped((8, LANES))],
        prefetch=1,
        vmem=10,
        flops=4 * CENT * CHUNK * 20,
        nbytes=4 << 20,
    )(z, g, kl, right, left)


def point_body(cent, hi, lo, csum, zt, out):
    c = cent[...]
    dims = (((0,), (0,)), ((), ()))
    g = lax.dot_general(c, hi[...], dims, preferred_element_type=F32)
    g = g + lax.dot_general(c, lo[...], dims, preferred_element_type=F32)
    total = jnp.sum(csum[...], axis=0, keepdims=True)
    v = total * zt[...].astype(F32) - g
    expo = exponent(v)
    for k in range(TILE // BLOCK):
        out[k, :, :ROWS] = code(v[k * BLOCK : (k + 1) * BLOCK, :], expo)
        out[k, :, ROWS:] = jnp.broadcast_to(expo, (BLOCK, LANES)).astype(BF16)


def point_call(centroids, hi, lo, csum, zt):
    block = (TILE // BLOCK, BLOCK, ROWS + LANES)
    return call(
        point_body,
        (D // TILE,),
        [
            pl.BlockSpec((CENT, TILE), lambda s: (0, s)),
            whole((CENT, ROWS)),
            whole((CENT, ROWS)),
            whole((8, ROWS)),
            pl.BlockSpec((TILE, ROWS), lambda s: (s, 0)),
        ],
        pl.BlockSpec(block, lambda s: (s, 0, 0)),
        shaped((NCENT, BLOCK, ROWS + LANES), BF16),
        vmem=18,
        flops=4 * CENT * ROWS * D,
        nbytes=18 << 20,
    )(in_hbm(centroids), hi, lo, csum, zt)


def point_sum_body(msgs, out):
    total = jnp.zeros(out.shape, F32)
    for k in range(NCENT):
        total = total + uncode(msgs[k, :, :ROWS], msgs[k, 0:1, ROWS : ROWS + 1].astype(F32))
    out[...] = total * SCALE


def point_sum_call(msgs):
    return call(
        point_sum_body,
        (1,),
        [whole(msgs.shape)],
        whole((BLOCK, ROWS)),
        shaped((BLOCK, ROWS)),
        vmem=10,
        flops=D * ROWS * 20,
        nbytes=3 << 20,
    )(msgs)


def gather_points(v):
    def stage(v, shifts):
        return jnp.stack([v] + [lax.ppermute(v, "cent", cent_shift(*d)) for d in shifts])

    v = stage(v, [(0, k, 0) for k in (1, 2, 3)])
    v = stage(v, [(k, 0, 0) for k in (1, 2, 3)])
    return v, lax.ppermute(v, "cent", cent_shift(0, 0, 1))


def per_device(points, centroids):
    me = lax.axis_index("cent")
    x, y, c = me // (NY * NC), (me // NC) % NY, me % NC
    at = jnp.stack([x, y, c]).astype(jnp.int32)
    zi = lax.axis_index("pts").astype(jnp.int32)
    z = zi[None]
    mine, other = gather_points(points.T)
    kern, norm, zt, zn = kern_call(at, mine, other, centroids)
    norms = lax.all_to_all(norm, "cent", 0, 0)
    freq, inv = freq_call(norms, kern)
    freqs = lax.all_to_all(freq, "pts", 0, 0)
    den = denom_call(freqs, inv, kern)
    dens = lax.all_to_all(den, "cent", 0, 0)
    hi, lo, csum, kl, g, ra, la = coef_call(z, dens, freqs, inv, kern, centroids, zn)

    def send(right, left):
        return lax.ppermute(right, "pts", z_shift(1)), lax.ppermute(left, "pts", z_shift(-1))

    got = send(ra, la)
    msgs = hop_call(z, g, kl, 3, got)
    hi, lo, right, left = lax.optimization_barrier((hi, lo, *msgs))
    got = send(right, left)
    pmsgs = point_call(centroids, hi, lo, csum, zt)
    pmsgs, right, left = lax.optimization_barrier((pmsgs, *got))
    got = (right, left)
    for k in (2, 1):
        got = send(*hop_call(z, g, kl, k, got))
    grad_centroids, loss = end_call(z, g, kl, *got)
    grad_points = point_sum_call(lax.all_to_all(pmsgs, "cent", 0, 0)).T
    return (grad_points, grad_centroids, loss[0, 0])


def solution(mesh):
    in_specs = (P("pts", "cent"), P("cent", None))
    out_specs = (P("pts", "cent"), P("cent", "pts"), P())
    return jax.shard_map(per_device, mesh=mesh, in_specs=in_specs, out_specs=out_specs, check_vma=False)
```

time: 453 us -> 188 us (0.42)
  blocking collectives: 217 us -> 30.8 us
  waiting for transfers between devices: 127 us -> 52.5 us
  matrix products: 57.8 us -> 0 us
  Pallas kernels: 0 us -> 56.7 us
  starting transfers between devices: 0.34 us -> 33.5 us
  other arithmetic: 30.2 us -> 1.09 us
  between operations: 15.6 us -> 0.87 us
  local copies, waits for them, and re-layouts: 3.23 us -> 11.5 us
    psum x4 -> x0, blocking collectives: 217 us -> none  [the longest x1 76.3 us: per_device(): kl_sum = lax.psum(kl_part, ('pts', 'cent'))]
    reduce_scatter x2 -> x0, waiting for transfers between devices: 75.9 us -> none  [the longest x1 75.9 us: per_device(): part = lax.psum_scatter(term_cent, 'pts', scatter_dimension=1, tiled=True)]
    dot_general x3 -> x0, matrix products: 57.8 us -> none  [the longest x1 30.9 us: per_device(): jnp.dot(coef.T, zfloat, precision=lax.Precision.HIGHEST)]
    pallas_call x0 -> x10, Pallas kernels: none -> 56.7 us  [the longest x1 14.3 us: coef_call(): call(coef_body, (WSTEPS,), [whole((NCENT, 16, LANES)), whole((NZ, CENT //...]
    all_gather x1 -> x0, waiting for transfers between devices: 50.8 us -> none  [per_device(): zrows = lax.all_gather(points, 'cent', axis=1, tiled=True)]
    ppermute x0 -> x15, waiting for transfers between devices: none -> 45 us  [the longest x4 30.1 us: send(): lax.ppermute(right, 'pts', z_shift(1))]
    all_to_all x0 -> x2, blocking collectives: none -> 30.8 us  [the longest x1 16.6 us: per_device(): freqs = lax.all_to_all(freq, 'pts', 0, 0)]
    reduce_sum x5 -> x0, other arithmetic: 26.4 us -> none  [the longest x1 10.6 us: per_device(): jnp.sum(coef, axis=0)[:, None] * cfloat]
  transfers between devices with their start and end apart: 3 -> 17, of which waited for: 2 -> 11; matrix products, arithmetic and copies ran while one was open for 8% -> 0% of each run, Pallas kernels for 0% -> 11%
where the time goes in v2:
time: 188 us; the launch traced here: 187 us
  Pallas kernels  56.7 us (30%)
  waiting for transfers between devices  52.5 us (28%)
  starting transfers between devices  33.5 us (18%)
  blocking collectives  30.8 us (16%)
  local copies, waits for them, and re-layouts  11.5 us (6%)
    ppermute x4, waiting for transfers between devices, send(): lax.ppermute(right, 'pts', z_shift(1))  30.1 us
    all_to_all x1, blocking collectives, per_device(): freqs = lax.all_to_all(freq, 'pts', 0, 0)  16.6 us
    pallas_call x1, Pallas kernels, coef_call(): call(coef_body, (WSTEPS,), [whole((NCENT, 16, LANES)), whole((NZ, CENT //...  14.3 us
    all_to_all x1, blocking collectives, per_device(): norms = lax.all_to_all(norm, 'cent', 0, 0)  14.1 us
    pallas_call x1, Pallas kernels, point_call(): call(point_body, (D // TILE,), [pl.BlockSpec((CENT, TILE), lambda s: (0,...  12.8 us
    ppermute x6, waiting for transfers between devices, stage(): lax.ppermute(v, 'cent', cent_shift(*d))  12.4 us
    ppermute x4, starting transfers between devices, send(): lax.ppermute(left, 'pts', z_shift(-1))  12.3 us
    pallas_call x1, Pallas kernels, kern_call(): call(kern_body, (WSTEPS,), [pl.BlockSpec(memory_space=pl.ANY), pl.BlockSp...  11.5 us
  transfers between devices with their start and end apart: 17, of which 11 were waited for; matrix products, arithmetic and copies ran while one was open for 0% of the time, Pallas kernels for 11%

profile of v2, /device:TPU:8, one launch (start us, length us, event | category | flops | bytes accessed | tf_op | source)
XLA Modules:
  0.0 186.9 jit_solution(4467002340218932004)
XLA Ops:
  0.6 2.4 %collective-permute-start.1 = (bf16[32,1024]{1,0:T(8,128)(2,1)}, bf16[32,1024]{1,0:T(8,128)(2,1)S(1)}, u32[]{:S(2)}, u32[]{:S(2)}) collective-permute-start(bf16[32,1024]{1,0:T(8,128)(2,1)} %bitcast.23), channel_id=1, source_target_pairs={{0,4},{1,5},{2,6},{3,7},{4,0},{5,1},{6,2},{7,3},{8,12},{9,13},{10,... | collective-permute-start | bytes 196616 | tf_op jit(solution)/shard_map/ppermute | solution.py:499
  3.0 1.4 collective-permute-start
  4.4 0.7 collective-permute-start.2
  5.0 1.7 collective-permute-done.1
  6.8 1.0 collective-permute-done
  7.8 1.1 collective-permute-done.2
  8.8 0.9 fusion
  9.7 2.1 %collective-permute-start.4 = (bf16[4,32,1024]{2,1,0:T(8,128)(2,1)S(1)}, bf16[4,32,1024]{2,1,0:T(8,128)(2,1)S(1)}, u32[]{:S(2)}, u32[]{:S(2)}) collective-permute-start(bf16[4,32,1024]{2,1,0:T(8,128)(2,1)S(1)} %get-tuple-element.60), channel_id=1, source_target_pairs={{0,16},{1,17},{2,18},{3,19},{4,20},{5,21},{6,22},{7,23},{8,24},{9,... | collective-permute-start | bytes 786440 | tf_op jit(solution)/shard_map/ppermute | solution.py:499
  11.8 0.6 collective-permute-start.3
  12.4 2.6 %collective-permute-start.5 = (bf16[4,32,1024]{2,1,0:T(8,128)(2,1)S(1)}, bf16[4,32,1024]{2,1,0:T(8,128)(2,1)S(1)}, u32[]{:S(2)}, u32[]{:S(2)}) collective-permute-start(bf16[4,32,1024]{2,1,0:T(8,128)(2,1)S(1)} %get-tuple-element.60), channel_id=1, source_target_pairs={{0,24},{1,25},{2,26},{3,27},{4,28},{5,29},{6,30},{7,31},{8,0},{9,1... | collective-permute-start | bytes 786440 | tf_op jit(solution)/shard_map/ppermute | solution.py:499
  15.0 5.5 %collective-permute-done.4 = bf16[4,32,1024]{2,1,0:T(8,128)(2,1)S(1)} collective-permute-done((bf16[4,32,1024]{2,1,0:T(8,128)(2,1)S(1)}, bf16[4,32,1024]{2,1,0:T(8,128)(2,1)S(1)}, u32[]{:S(2)}, u32[]{:S(2)}) %collective-permute-start.4) | collective-permute-done | bytes 262176 | tf_op jit(solution)/shard_map/ppermute | solution.py:499
  20.5 2.8 %collective-permute-done.3 = bf16[4,32,1024]{2,1,0:T(8,128)(2,1)S(1)} collective-permute-done((bf16[4,32,1024]{2,1,0:T(8,128)(2,1)S(1)}, bf16[4,32,1024]{2,1,0:T(8,128)(2,1)S(1)}, u32[]{:S(2)}, u32[]{:S(2)}) %collective-permute-start.3) | collective-permute-done | bytes 262176 | tf_op jit(solution)/shard_map/ppermute | solution.py:499
  23.3 0.3 collective-permute-done.5
  23.6 0.1 pad_maximum_fusion.mine
  23.7 0.1 collective-permute-start.6
  23.9 2.5 %collective-permute-done.6.other = bf16[4,4,32,1024]{3,2,1,0:T(8,128)(2,1)S(1)} collective-permute-done((bf16[4,4,32,1024]{3,2,1,0:T(8,128)(2,1)S(1)}, bf16[4,4,32,1024]{3,2,1,0:T(8,128)(2,1)S(1)}, u32[]{:S(2)}, u32[]{:S(2)}) %collective-permute-start.6) | collective-permute-done | bytes 1048608 | tf_op jit(solution)/shard_map/ppermute | solution.py:503
  26.5 11.5 %shard_map.49 = (f32[2048,1024]{1,0:T(8,128)S(1)}, f32[32,8,128]{2,1,0:T(8,128)S(1)}, bf16[1024,1024]{1,0:T(8,128)(2,1)S(1)}, bf16[1024,1024]{1,0:T(8,128)(2,1)S(1)}) custom-call(s32[3]{0:T(128)S(1)} %pad_add_fusion.at, bf16[4,4,32,1024]{3,2,1,0:T(8,128)(2,1)S(1)} %pad_maximum_fusion.mine, bf16[4,4,32,1024]{3,2,1,0:T(8,128)(2,1)S(1)} %collective-permute-done.6.other, ...), custom_call_target="tpu_custom_call" | custom-call | flops 4294967296 | bytes 20971520 | tf_op jit(solution)/shard_map/pallas_call | solution.py:159
  38.0 1.4 copy-done.5
  39.3 1.4 copy-done.7
  40.7 14.1 %all_to_all.20.norms = f32[32,8,128]{2,1,0:T(8,128)S(1)} all-to-all(f32[32,8,128]{2,1,0:T(8,128)S(1)} %get-tuple-element.31), channel_id=1, replica_groups=mesh['pts'=8,'cent'=32] {'cent'}, dimensions={0} | all-to-all | bytes 262144 | tf_op jit(solution)/shard_map/all_to_all | solution.py:514
  54.8 1.3 shard_map.50
  56.2 16.6 %all_to_all.21.freqs = f32[8,16,128]{2,1,0:T(8,128)S(1)} all-to-all(f32[8,16,128]{2,1,0:T(8,128)S(1)} %get-tuple-element.33), channel_id=1, replica_groups=mesh['pts'=8,'cent'=32] {'pts'}, dimensions={0} | all-to-all | bytes 131072 | tf_op jit(solution)/shard_map/all_to_all | solution.py:516
  72.8 3.9 %shard_map.51 = f32[32,16,128]{2,1,0:T(8,128)} custom-call(f32[8,16,128]{2,1,0:T(8,128)S(1)} %all_to_all.21.freqs, f32[8,128]{1,0:T(8,128)S(1)} %get-tuple-element.34.inv, f32[2048,1024]{1,0:T(8,128)S(1)} %get-tuple-element.32.kern), custom_call_target="tpu_custom_call" | custom-call | flops 12582912 | bytes 8388608 | tf_op jit(solution)/shard_map/pallas_call | solution.py:240
  76.7 5.0 %all-to-all-start.2 = ((f32[32,16,128]{2,1,0:T(8,128)}), f32[32,16,128]{2,1,0:T(8,128)S(1)}, u32[]{:S(2)}, u32[]{:S(2)}) async-start(f32[32,16,128]{2,1,0:T(8,128)} %shard_map.51), calls=%async_computation.2 | async-start | bytes 524288 | tf_op jit(solution)/shard_map/all_to_all | solution.py:518
  81.7 7.4 %all-to-all-done.2.dens = f32[32,16,128]{2,1,0:T(8,128)S(1)} async-done(((f32[32,16,128]{2,1,0:T(8,128)}), f32[32,16,128]{2,1,0:T(8,128)S(1)}, u32[]{:S(2)}, u32[]{:S(2)}) %all-to-all-start.2) | async-done | bytes 262176 | tf_op jit(solution)/shard_map/all_to_all | solution.py:518
  89.2 3.4 %copy-done.3 = f32[2048,1024]{1,0:T(8,128)S(1)} copy-done((f32[2048,1024]{1,0:T(8,128)S(1)}, f32[2048,1024]{1,0:T(8,128)}, u32[]{:S(2)}) %copy-start.3) | copy-done | bytes 8388632
  92.6 14.3 %shard_map.52 = (bf16[2048,1024]{1,0:T(8,128)(2,1)S(1)}, bf16[2048,1024]{1,0:T(8,128)(2,1)S(1)}, f32[8,1024]{1,0:T(8,128)S(1)}, f32[8,128]{1,0:T(8,128)S(1)}, f3...) custom-call(s32[1]{0:T(128)} %bitcast.z.at, ...), custom_call_target="tpu_custom_call" | custom-call | flops 8589934592 | bytes 31457280 | tf_op jit(solution)/shard_map/pallas_call | solution.py:350
  106.9 0.8 collective-permute-start.7
  107.7 2.7 %collective-permute-start.8 = (bf16[1040,128]{1,0:T(8,128)(2,1)S(1)}, bf16[1040,128]{1,0:T(8,128)(2,1)S(1)}, u32[]{:S(2)}, u32[]{:S(2)}) collective-permute-start(bf16[1040,128]{1,0:T(8,128)(2,1)S(1)} %get-tuple-element.41), channel_id=1, source_target_pairs={{0,224},{32,0},{64,32},{96,64},{128,96},{160,128},{192,160},{224,1... | collective-permute-start | bytes 798728 | tf_op jit(solution)/shard_map/ppermute | solution.py:522
  110.4 6.9 %collective-permute-done.7.got_right = bf16[1040,128]{1,0:T(8,128)(2,1)S(1)} collective-permute-done((bf16[1040,128]{1,0:T(8,128)(2,1)S(1)}, bf16[1040,128]{1,0:T(8,128)(2,1)S(1)}, u32[]{:S(2)}, u32[]{:S(2)}) %collective-permute-start.7) | collective-permute-done | bytes 266272 | tf_op jit(solution)/shard_map/ppermute | solution.py:522
  117.3 2.0 %shard_map.53 = (bf16[2064,128]{1,0:T(8,128)(2,1)S(1)}, bf16[2064,128]{1,0:T(8,128)(2,1)S(1)}) custom-call(s32[1]{0:T(128)} %bitcast.z.at, f32[8,2048,128]{2,1,0:T(8,128)S(1)} %get-tuple-element.38.a.b.own, f32[8,2048,128]{2,1,0:T(8,128)S(1)} %get-tuple-element.38.a.b.own, f32[8,128]{1,0:T(8,128)S(1)} %get-tuple-element.39.kl, ...), custom_call_target="tpu_custom_call" | custom-call | flops 41943040 | bytes 3145728 | tf_op jit(solution)/shard_map/pallas_call | solution.py:410
  119.3 0.1 collective-permute-start.9
  119.4 3.2 %collective-permute-start.10 = (bf16[2064,128]{1,0:T(8,128)(2,1)S(1)}, bf16[2064,128]{1,0:T(8,128)(2,1)S(1)}, u32[]{:S(2)}, u32[]{:S(2)}) collective-permute-start(bf16[2064,128]{1,0:T(8,128)(2,1)S(1)} %get-tuple-element.49), channel_id=1, source_target_pairs={{0,224},{32,0},{64,32},{96,64},{128,96},{160,128},{192,160},{224,1... | collective-permute-start | bytes 1585160 | tf_op jit(solution)/shard_map/ppermute | solution.py:522
  122.6 12.8 %shard_map.54 = bf16[32,32,1152]{2,1,0:T(8,128)(2,1)S(1)} custom-call(bf16[2048,1024]{1,0:T(8,128)(2,1)} %cent.5, bf16[2048,1024]{1,0:T(8,128)(2,1)S(1)} %get-tuple-element.44.hi, bf16[2048,1024]{1,0:T(8,128)(2,1)S(1)} %get-tuple-element.45.lo, f32[8,1024]{1,0:T(8,128)S(1)} %get-tuple-element.46.csum, bf16[1024,1024]{1,0:T(8,128)(2,1)S(1)} %copy-done.6), custom_call_target="tpu_custom_call" | custom-call | flops 8589934592 | bytes 18874368 | tf_op jit(solution)/shard_map/pallas_call | solution.py:459
  135.4 1.4 copy-done.4
  136.9 5.3 %all-to-all-start.3 = ((bf16[32,32,1152]{2,1,0:T(8,128)(2,1)}), bf16[32,32,1152]{2,1,0:T(8,128)(2,1)S(1)}, u32[]{:S(2)}, u32[]{:S(2)}) async-start(bf16[32,32,1152]{2,1,0:T(8,128)(2,1)} %copy-done.4), calls=%async_computation.3 | async-start | bytes 4718592 | tf_op jit(solution)/shard_map/all_to_all | solution.py:534
  142.1 3.4 %copy-done.1 = f32[8,2048,128]{2,1,0:T(8,128)S(1)} copy-done((f32[8,2048,128]{2,1,0:T(8,128)S(1)}, f32[8,2048,128]{2,1,0:T(8,128)}, u32[]{:S(2)}) %copy-start.1) | copy-done | bytes 8388632
  145.5 2.7 %shard_map.56 = (bf16[2064,128]{1,0:T(8,128)(2,1)S(1)}, bf16[2064,128]{1,0:T(8,128)(2,1)S(1)}) custom-call(s32[1]{0:T(128)} %bitcast.z.at, f32[8,2048,128]{2,1,0:T(8,128)S(1)} %copy-done.1, f32[8,2048,128]{2,1,0:T(8,128)S(1)} %copy-done.1, f32[8,128]{1,0:T(8,128)S(1)} %get-tuple-element.39.kl, bf16[2064,128]{1,0:T(8,128)(2,1)S(1)} %collective-permute-done.9.got_right, ...), custom_call_target="tpu_custom_call" | custom-call | flops 41943040 | bytes 3145728 | tf_op jit(solution)/shard_map/pallas_call | solution.py:410
  148.2 0.1 collective-permute-start.11
  148.3 3.2 %collective-permute-start.12 = (bf16[2064,128]{1,0:T(8,128)(2,1)S(1)}, bf16[2064,128]{1,0:T(8,128)(2,1)S(1)}, u32[]{:S(2)}, u32[]{:S(2)}) collective-permute-start(bf16[2064,128]{1,0:T(8,128)(2,1)S(1)} %get-tuple-element.54), channel_id=1, source_target_pairs={{0,224},{32,0},{64,32},{96,64},{128,96},{160,128},{192,160},{224,1... | collective-permute-start | bytes 1585160 | tf_op jit(solution)/shard_map/ppermute | solution.py:522
  151.5 12.0 %collective-permute-done.11.got_right = bf16[2064,128]{1,0:T(8,128)(2,1)S(1)} collective-permute-done((bf16[2064,128]{1,0:T(8,128)(2,1)S(1)}, bf16[2064,128]{1,0:T(8,128)(2,1)S(1)}, u32[]{:S(2)}, u32[]{:S(2)}) %collective-permute-start.11) | collective-permute-done | bytes 528416 | tf_op jit(solution)/shard_map/ppermute | solution.py:522
  163.5 2.7 %shard_map.57 = (bf16[2064,128]{1,0:T(8,128)(2,1)S(1)}, bf16[2064,128]{1,0:T(8,128)(2,1)S(1)}) custom-call(s32[1]{0:T(128)} %bitcast.z.at, f32[8,2048,128]{2,1,0:T(8,128)S(1)} %copy-done.1, f32[8,2048,128]{2,1,0:T(8,128)S(1)} %copy-done.1, f32[8,128]{1,0:T(8,128)S(1)} %get-tuple-element.39.kl, bf16[2064,128]{1,0:T(8,128)(2,1)S(1)} %collective-permute-done.11.got_right, ...), custom_call_target="tpu_custom_call" | custom-call | flops 41943040 | bytes 3145728 | tf_op jit(solution)/shard_map/pallas_call | solution.py:410
  166.2 0.1 collective-permute-start.13
  166.3 3.2 %collective-permute-start.14 = (bf16[2064,128]{1,0:T(8,128)(2,1)S(1)}, bf16[2064,128]{1,0:T(8,128)(2,1)S(1)}, u32[]{:S(2)}, u32[]{:S(2)}) collective-permute-start(bf16[2064,128]{1,0:T(8,128)(2,1)S(1)} %get-tuple-element.56), channel_id=1, source_target_pairs={{0,224},{32,0},{64,32},{96,64},{128,96},{160,128},{192,160},{224,1... | collective-permute-start | bytes 1585160 | tf_op jit(solution)/shard_map/ppermute | solution.py:522
  169.5 11.2 %collective-permute-done.13.right = bf16[2064,128]{1,0:T(8,128)(2,1)S(1)} collective-permute-done((bf16[2064,128]{1,0:T(8,128)(2,1)S(1)}, bf16[2064,128]{1,0:T(8,128)(2,1)S(1)}, u32[]{:S(2)}, u32[]{:S(2)}) %collective-permute-start.13) | collective-permute-done | bytes 528416 | tf_op jit(solution)/shard_map/ppermute | solution.py:522
  180.7 2.6 %shard_map.58 = (f32[2048,128]{1,0:T(8,128)}, f32[8,128]{1,0:T(8,128)S(1)}) custom-call(s32[1]{0:T(128)} %bitcast.z.at, f32[8,2048,128]{2,1,0:T(8,128)S(1)} %bitcast.18, f32[8,128]{1,0:T(8,128)S(1)} %get-tuple-element.39.kl, bf16[2064,128]{1,0:T(8,128)(2,1)S(1)} %collective-permute-done.13.right, bf16[2064,128]{1,0:T(8,128)(2,1)S(1)} %collective-permute-done.14.left), custom_call_target="tpu_custom_call" | custom-call | flops 20971520 | bytes 4194304 | tf_op jit(solution)/shard_map/pallas_call | solution.py:431
  183.3 0.5 slice.3
  183.8 3.0 %shard_map.55 = f32[32,1024]{1,0:T(8,128)} custom-call(bf16[32,32,1152]{2,1,0:T(8,128)(2,1)S(1)} %all-to-all-done.3.msgs), custom_call_target="tpu_custom_call" | custom-call | flops 20971520 | bytes 3145728 | tf_op jit(solution)/shard_map/pallas_call | solution.py:485
  (25 shorter events, 0.1 us)
Async XLA Ops:
  0.6 6.1 %collective-permute-start.1 = (bf16[32,1024]{1,0:T(8,128)(2,1)}, bf16[32,1024]{1,0:T(8,128)(2,1)S(1)}, u32[]{:S(2)}, u32[]{:S(2)}) collective-permute-start(bf16[32,1024]{1,0:T(8,128)(2,1)} %bitcast.23), channel_id=1, source_target_pairs={{0,4},{1,5},{2,6},{3,7},{4,0},{5,1},{6,2},{7,3},{8,12},{9,13},{10,... | collective-permute-start | bytes 196616 | tf_op jit(solution)/shard_map/ppermute | solution.py:499
  3.0 4.8 %collective-permute-start = (bf16[32,1024]{1,0:T(8,128)(2,1)}, bf16[32,1024]{1,0:T(8,128)(2,1)S(1)}, u32[]{:S(2)}, u32[]{:S(2)}) collective-permute-start(bf16[32,1024]{1,0:T(8,128)(2,1)} %bitcast.24), channel_id=1, source_target_pairs={{0,2},{1,3},{2,4},{3,5},{4,6},{5,7},{6,0},{7,1},{8,10},{9,11},{10,... | collective-permute-start | bytes 196616 | tf_op jit(solution)/shard_map/ppermute | solution.py:499
  4.4 4.5 %collective-permute-start.2 = (bf16[32,1024]{1,0:T(8,128)(2,1)}, bf16[32,1024]{1,0:T(8,128)(2,1)S(1)}, u32[]{:S(2)}, u32[]{:S(2)}) collective-permute-start(bf16[32,1024]{1,0:T(8,128)(2,1)} %bitcast.25), channel_id=1, source_target_pairs={{0,6},{1,7},{2,0},{3,1},{4,2},{5,3},{6,4},{7,5},{8,14},{9,15},{10,... | collective-permute-start | bytes 196616 | tf_op jit(solution)/shard_map/ppermute | solution.py:499
  9.7 10.8 %collective-permute-start.4 = (bf16[4,32,1024]{2,1,0:T(8,128)(2,1)S(1)}, bf16[4,32,1024]{2,1,0:T(8,128)(2,1)S(1)}, u32[]{:S(2)}, u32[]{:S(2)}) collective-permute-start(bf16[4,32,1024]{2,1,0:T(8,128)(2,1)S(1)} %get-tuple-element.60), channel_id=1, source_target_pairs={{0,16},{1,17},{2,18},{3,19},{4,20},{5,21},{6,22},{7,23},{8,24},{9,... | collective-permute-start | bytes 786440 | tf_op jit(solution)/shard_map/ppermute | solution.py:499
  11.8 11.5 %collective-permute-start.3 = (bf16[4,32,1024]{2,1,0:T(8,128)(2,1)S(1)}, bf16[4,32,1024]{2,1,0:T(8,128)(2,1)S(1)}, u32[]{:S(2)}, u32[]{:S(2)}) collective-permute-start(bf16[4,32,1024]{2,1,0:T(8,128)(2,1)S(1)} %get-tuple-element.60), channel_id=1, source_target_pairs={{0,8},{1,9},{2,10},{3,11},{4,12},{5,13},{6,14},{7,15},{8,16},{9,17... | collective-permute-start | bytes 786440 | tf_op jit(solution)/shard_map/ppermute | solution.py:499
  12.4 11.2 %collective-permute-start.5 = (bf16[4,32,1024]{2,1,0:T(8,128)(2,1)S(1)}, bf16[4,32,1024]{2,1,0:T(8,128)(2,1)S(1)}, u32[]{:S(2)}, u32[]{:S(2)}) collective-permute-start(bf16[4,32,1024]{2,1,0:T(8,128)(2,1)S(1)} %get-tuple-element.60), channel_id=1, source_target_pairs={{0,24},{1,25},{2,26},{3,27},{4,28},{5,29},{6,30},{7,31},{8,0},{9,1... | collective-permute-start | bytes 786440 | tf_op jit(solution)/shard_map/ppermute | solution.py:499
  23.7 2.7 %collective-permute-start.6 = (bf16[4,4,32,1024]{3,2,1,0:T(8,128)(2,1)S(1)}, bf16[4,4,32,1024]{3,2,1,0:T(8,128)(2,1)S(1)}, u32[]{:S(2)}, u32[]{:S(2)}) collective-permute-start(bf16[4,4,32,1024]{3,2,1,0:T(8,128)(2,1)S(1)} %pad_maximum_fusion.mine), channel_id=1, source_target_pairs={{0,1},{1,0},{2,3},{3,2},{4,5},{5,4},{6,7},{7,6},{8,9},{9,8},{10,11... | collective-permute-start | bytes 3145736 | tf_op jit(solution)/shard_map/ppermute | solution.py:503
  38.0 1.4 copy-start.5
  39.3 1.4 copy-start.7
  40.7 32.1 %copy-start.2 = (f32[2048,1024]{1,0:T(8,128)}, f32[2048,1024]{1,0:T(8,128)S(1)}, u32[]{:S(2)}) copy-start(f32[2048,1024]{1,0:T(8,128)S(1)} %get-tuple-element.32.kern) | copy-start | bytes 25165828
  72.8 16.4 %copy-start.8 = (bf16[1024,1024]{1,0:T(8,128)(2,1)S(1)}, bf16[1024,1024]{1,0:T(8,128)(2,1)}, u32[]{:S(2)}) copy-start(bf16[1024,1024]{1,0:T(8,128)(2,1)} %copy-done.7) | copy-start | bytes 6291460
  76.7 12.5 %all-to-all-start.2 = ((f32[32,16,128]{2,1,0:T(8,128)}), f32[32,16,128]{2,1,0:T(8,128)S(1)}, u32[]{:S(2)}, u32[]{:S(2)}) async-start(f32[32,16,128]{2,1,0:T(8,128)} %shard_map.51), calls=%async_computation.2 | async-start | bytes 524288 | tf_op jit(solution)/shard_map/all_to_all | solution.py:518
  89.2 3.4 %copy-start.3 = (f32[2048,1024]{1,0:T(8,128)S(1)}, f32[2048,1024]{1,0:T(8,128)}, u32[]{:S(2)}) copy-start(f32[2048,1024]{1,0:T(8,128)} %copy-done.2) | copy-start | bytes 25165828
  106.9 12.4 %copy-start = (f32[8,2048,128]{2,1,0:T(8,128)}, f32[8,2048,128]{2,1,0:T(8,128)S(1)}, u32[]{:S(2)}) copy-start(f32[8,2048,128]{2,1,0:T(8,128)S(1)} %get-tuple-element.38.a.b.own) | copy-start | bytes 25165828
  106.9 10.4 %collective-permute-start.7 = (bf16[1040,128]{1,0:T(8,128)(2,1)S(1)}, bf16[1040,128]{1,0:T(8,128)(2,1)S(1)}, u32[]{:S(2)}, u32[]{:S(2)}) collective-permute-start(bf16[1040,128]{1,0:T(8,128)(2,1)S(1)} %get-tuple-element.40), channel_id=1, source_target_pairs={{0,32},{32,64},{64,96},{96,128},{128,160},{160,192},{192,224},{224... | collective-permute-start | bytes 798728 | tf_op jit(solution)/shard_map/ppermute | solution.py:522
  107.7 9.6 %collective-permute-start.8 = (bf16[1040,128]{1,0:T(8,128)(2,1)S(1)}, bf16[1040,128]{1,0:T(8,128)(2,1)S(1)}, u32[]{:S(2)}, u32[]{:S(2)}) collective-permute-start(bf16[1040,128]{1,0:T(8,128)(2,1)S(1)} %get-tuple-element.41), channel_id=1, source_target_pairs={{0,224},{32,0},{64,32},{96,64},{128,96},{160,128},{192,160},{224,1... | collective-permute-start | bytes 798728 | tf_op jit(solution)/shard_map/ppermute | solution.py:522
  117.3 5.3 %copy-start.6 = (bf16[1024,1024]{1,0:T(8,128)(2,1)S(1)}, bf16[1024,1024]{1,0:T(8,128)(2,1)}, u32[]{:S(2)}) copy-start(bf16[1024,1024]{1,0:T(8,128)(2,1)} %copy-done.5) | copy-start | bytes 6291460
  119.3 17.6 %collective-permute-start.9 = (bf16[2064,128]{1,0:T(8,128)(2,1)S(1)}, bf16[2064,128]{1,0:T(8,128)(2,1)S(1)}, u32[]{:S(2)}, u32[]{:S(2)}) collective-permute-start(bf16[2064,128]{1,0:T(8,128)(2,1)S(1)} %get-tuple-element.48), channel_id=1, source_target_pairs={{0,32},{32,64},{64,96},{96,128},{128,160},{160,192},{192,224},{224... | collective-permute-start | bytes 1585160 | tf_op jit(solution)/shard_map/ppermute | solution.py:522
  119.4 17.5 %collective-permute-start.10 = (bf16[2064,128]{1,0:T(8,128)(2,1)S(1)}, bf16[2064,128]{1,0:T(8,128)(2,1)S(1)}, u32[]{:S(2)}, u32[]{:S(2)}) collective-permute-start(bf16[2064,128]{1,0:T(8,128)(2,1)S(1)} %get-tuple-element.49), channel_id=1, source_target_pairs={{0,224},{32,0},{64,32},{96,64},{128,96},{160,128},{192,160},{224,1... | collective-permute-start | bytes 1585160 | tf_op jit(solution)/shard_map/ppermute | solution.py:522
  135.4 1.4 copy-start.4
  136.9 47.0 %all-to-all-start.3 = ((bf16[32,32,1152]{2,1,0:T(8,128)(2,1)}), bf16[32,32,1152]{2,1,0:T(8,128)(2,1)S(1)}, u32[]{:S(2)}, u32[]{:S(2)}) async-start(bf16[32,32,1152]{2,1,0:T(8,128)(2,1)} %copy-done.4), calls=%async_computation.3 | async-start | bytes 4718592 | tf_op jit(solution)/shard_map/all_to_all | solution.py:534
  142.1 3.4 %copy-start.1 = (f32[8,2048,128]{2,1,0:T(8,128)S(1)}, f32[8,2048,128]{2,1,0:T(8,128)}, u32[]{:S(2)}) copy-start(f32[8,2048,128]{2,1,0:T(8,128)} %copy-done) | copy-start | bytes 25165828
  148.2 15.4 %collective-permute-start.11 = (bf16[2064,128]{1,0:T(8,128)(2,1)S(1)}, bf16[2064,128]{1,0:T(8,128)(2,1)S(1)}, u32[]{:S(2)}, u32[]{:S(2)}) collective-permute-start(bf16[2064,128]{1,0:T(8,128)(2,1)S(1)} %get-tuple-element.53), channel_id=1, source_target_pairs={{0,32},{32,64},{64,96},{96,128},{128,160},{160,192},{192,224},{224... | collective-permute-start | bytes 1585160 | tf_op jit(solution)/shard_map/ppermute | solution.py:522
  148.3 32.5 %slice-start = ((s8[8388608]{0:T(1024)(128)(4,1)}), s8[4194304]{0:T(1024)(128)(4,1)S(1)}, s32[]{:S(2)}) async-start(s8[8388608]{0:T(1024)(128)(4,1)} %bitcast.17), calls=%async_computation.4 | async-start | bytes 8388608
  148.3 32.4 %slice-start.1 = ((s8[8388608]{0:T(1024)(128)(4,1)}), s8[4194304]{0:T(1024)(128)(4,1)S(1)}, s32[]{:S(2)}) async-start(s8[8388608]{0:T(1024)(128)(4,1)} %bitcast.17), calls=%async_computation.5 | async-start | bytes 8388608
  148.3 15.2 %collective-permute-start.12 = (bf16[2064,128]{1,0:T(8,128)(2,1)S(1)}, bf16[2064,128]{1,0:T(8,128)(2,1)S(1)}, u32[]{:S(2)}, u32[]{:S(2)}) collective-permute-start(bf16[2064,128]{1,0:T(8,128)(2,1)S(1)} %get-tuple-element.54), channel_id=1, source_target_pairs={{0,224},{32,0},{64,32},{96,64},{128,96},{160,128},{192,160},{224,1... | collective-permute-start | bytes 1585160 | tf_op jit(solution)/shard_map/ppermute | solution.py:522
  166.2 14.5 %collective-permute-start.13 = (bf16[2064,128]{1,0:T(8,128)(2,1)S(1)}, bf16[2064,128]{1,0:T(8,128)(2,1)S(1)}, u32[]{:S(2)}, u32[]{:S(2)}) collective-permute-start(bf16[2064,128]{1,0:T(8,128)(2,1)S(1)} %get-tuple-element.55), channel_id=1, source_target_pairs={{0,32},{32,64},{64,96},{96,128},{128,160},{160,192},{192,224},{224... | collective-permute-start | bytes 1585160 | tf_op jit(solution)/shard_map/ppermute | solution.py:522
  166.3 14.4 %collective-permute-start.14 = (bf16[2064,128]{1,0:T(8,128)(2,1)S(1)}, bf16[2064,128]{1,0:T(8,128)(2,1)S(1)}, u32[]{:S(2)}, u32[]{:S(2)}) collective-permute-start(bf16[2064,128]{1,0:T(8,128)(2,1)S(1)} %get-tuple-element.56), channel_id=1, source_target_pairs={{0,224},{32,0},{64,32},{96,64},{128,96},{160,128},{192,160},{224,1... | collective-permute-start | bytes 1585160 | tf_op jit(solution)/shard_map/ppermute | solution.py:522

commit v3 on v2

--- a/solution.py
+++ b/solution.py
@@ -106,29 +106,42 @@
     return jax.ShapeDtypeStruct(shape, dtype)
 
 
-def kern_body(at, mine, other, cent, kern, norm, zt, zn, zsq, acc, sems):
+def kern_body(at, mine, other, cent, kern, norm, zt_out, zn_out, zt, zn, zsq, acc, sems, osems):
     step = pl.program_id(0)
+    copies = []
+    for cr in range(NC):
+        src = (mine, other)[cr]
+        for xr in range(NX):
+            for yr in range(NY):
+                xx = lax.rem(at[0] + NX - xr, NX)
+                yy = lax.rem(at[1] + NY - yr, NY)
+                cc = lax.rem(at[2] + cr, NC)
+                row = pl.multiple_of(((xx * NY + yy) * NC + cc) * BLOCK, BLOCK)
+                copies.append(
+                    pltpu.make_async_copy(
+                        src.at[xr, yr], zt.at[pl.ds(row, BLOCK), :], sems.at[(cr * NX + xr) * NY + yr]
+                    )
+                )
 
     @pl.when(step == 0)
     def _():
-        copies = []
-        for cr in range(NC):
-            src = (mine, other)[cr]
-            for xr in range(NX):
-                for yr in range(NY):
-                    xx = lax.rem(at[0] + NX - xr, NX)
-                    yy = lax.rem(at[1] + NY - yr, NY)
-                    cc = lax.rem(at[2] + cr, NC)
-                    row = pl.multiple_of(((xx * NY + yy) * NC + cc) * BLOCK, BLOCK)
-                    copies.append(
-                        pltpu.make_async_copy(
-                            src.at[xr, yr], zt.at[pl.ds(row, BLOCK), :], sems.at[(cr * NX + xr) * NY + yr]
-                        )
-                    )
         for cp in copies:
             cp.start()
+
+    c = cent[...]
+    cf = c.astype(F32)
+    msq = jnp.sum(lane_fold(cf * cf), axis=1, keepdims=True)
+    part = D // WSTEPS
+    outs = [pltpu.make_async_copy(zt, zt_out, osems.at[WSTEPS])]
+    for t in range(WSTEPS):
+        cols = pl.ds(t * part, part)
+        outs.append(pltpu.make_async_copy(zn.at[:, cols], zn_out.at[:, cols], osems.at[t]))
+
+    @pl.when(step == 0)
+    def _():
         for cp in copies:
             cp.wait()
+        outs[0].start()
         total = jnp.zeros((8, ROWS), F32)
         for k in range(D // LANES):
             v = zt[k * LANES : (k + 1) * LANES, :].astype(F32)
@@ -137,46 +150,52 @@
         zsq[...] = 1.0 + jnp.sum(total, axis=0, keepdims=True)
         acc[...] = jnp.zeros_like(acc)
 
-    c = cent[...]
-    cf = c.astype(F32)
-    msq = jnp.sum(lane_fold(cf * cf), axis=1, keepdims=True)
     for k in range(ROWS // SLAB):
         cols = slice(k * SLAB, (k + 1) * SLAB)
         dots = dot(c, zt[:, cols])
         v = 1.0 / ((zsq[:, cols] + msq) - 2.0 * dots)
         kern[:, cols] = v
         acc[:, cols] += jnp.sum(v.reshape(WIDE // 8, 8, SLAB), axis=0)
-    part = D // WSTEPS
-    first = pl.multiple_of(step * part, part)
-    zn[:, pl.ds(first, part)] = jnp.transpose(zt[pl.ds(first, part), :])
+    for t in range(WSTEPS):
+
+        @pl.when(step == t)
+        def _(t=t):
+            zn[:, t * part : (t + 1) * part] = jnp.transpose(zt[t * part : (t + 1) * part, :])
+            outs[1 + t].start()
 
     @pl.when(step == WSTEPS - 1)
     def _():
         store_tile(norm, jnp.sum(acc[...], axis=0, keepdims=True), NCENT, 0)
+        for cp in outs:
+            cp.wait()
 
 
 def kern_call(at, mine, other, centroids):
+    hbm = pl.BlockSpec(memory_space=pl.ANY)
     return call(
         kern_body,
         (WSTEPS,),
-        [
-            pl.BlockSpec(memory_space=pl.ANY),
-            pl.BlockSpec(memory_space=pl.ANY),
-            pl.BlockSpec((WIDE, D), lambda s, *_: (s, 0)),
-        ],
-        [
-            pl.BlockSpec((WIDE, ROWS), lambda s, *_: (s, 0)),
-            whole((NCENT, 8, LANES)),
-            whole((D, ROWS)),
-            whole((ROWS, D)),
-        ],
-        [shaped((CENT, ROWS)), shaped((NCENT, 8, LANES)), shaped((D, ROWS), BF16), shaped((ROWS, D), BF16)],
-        [pltpu.VMEM((1, ROWS), F32), pltpu.VMEM((8, ROWS), F32), pltpu.SemaphoreType.DMA((NCENT,))],
+        [hbm, hbm, pl.BlockSpec((WIDE, D), lambda s, *_: (s, 0))],
+        [pl.BlockSpec((WIDE, ROWS), lambda s, *_: (s, 0)), whole((NCENT, 8, LANES)), hbm, hbm],
+        [
+            shaped((CENT, ROWS)),
+            shaped((NCENT, 8, LANES)),
+            pltpu.HBM((D, ROWS), BF16),
+            pltpu.HBM((ROWS, D), BF16),
+        ],
+        [
+            pltpu.VMEM((D, ROWS), BF16),
+            pltpu.VMEM((ROWS, D), BF16),
+            pltpu.VMEM((1, ROWS), F32),
+            pltpu.VMEM((8, ROWS), F32),
+            pltpu.SemaphoreType.DMA((NCENT,)),
+            pltpu.SemaphoreType.DMA((WSTEPS + 1,)),
+        ],
         prefetch=1,
-        vmem=14,
+        vmem=18,
         flops=2 * CENT * ROWS * D,
         nbytes=20 << 20,
-    )(at, mine, other, in_hbm(centroids))
+    )(at, mine, in_hbm(other), in_hbm(centroids))
 
 
 def freq_body(norms, kern, freq, inv, row):
@@ -299,11 +318,15 @@
 FIRST = (HALF + PAD, CHUNK)
 
 
-def coef_body(z, dens, freqs, inv, kern, cent, zn, hi, lo, csum, kl, g, right, left, rf, row, rden, first):
+def coef_body(z, dens, freqs, inv, kern, cent, zn_hbm, hi, lo, csum, kl, g, right, left, rf, row, rden, first, zn, sem):
     step = pl.program_id(0)
+    rows = [pl.ds(q * (ROWS // 4), ROWS // 4) for q in range(4)]
+    loads = [pltpu.make_async_copy(zn_hbm.at[r], zn.at[r], sem.at[q]) for q, r in enumerate(rows)]
 
     @pl.when(step == 0)
     def _():
+        for cp in loads:
+            cp.start()
         rf[...] = 1.0 / jnp.sum(freqs[...], axis=0)
         row[...] = as_row(inv[...])
         both = jnp.sum(dens[...], axis=0)
@@ -330,6 +353,13 @@
         total = total + jnp.sum(coef.reshape(TILE // 8, 8, ROWS), axis=0)
         e = jnp.sum(lane_fold(coef), axis=1, keepdims=True)
         both = jnp.concatenate([h, l], axis=0)
+        if sub == 0:
+
+            @pl.when(step == 0)
+            def _():
+                for cp in loads:
+                    cp.wait()
+
         for n in range(D // SLAB):
             cols = slice(n * SLAB, (n + 1) * SLAB)
             r = dot(both, zn[:, cols])
@@ -356,7 +386,7 @@
             whole((8, LANES)),
             tiles,
             pl.BlockSpec((WIDE, D), lambda s, z: (s, 0)),
-            whole((ROWS, D)),
+            pl.BlockSpec(memory_space=pl.ANY),
         ],
         [
             tiles,
@@ -372,7 +402,7 @@
             shaped((CENT, ROWS), BF16),
             shaped((8, ROWS)),
             shaped((8, LANES)),
-            shaped((NZ, CENT, CHUNK)),
+            pltpu.HBM((NZ, CENT, CHUNK), F32),
             shaped(FIRST, BF16),
             shaped(FIRST, BF16),
         ],
@@ -381,67 +411,89 @@
             pltpu.VMEM((1, ROWS), F32),
             pltpu.VMEM((1, ROWS), F32),
             pltpu.VMEM((CENT, CHUNK), F32),
+            pltpu.VMEM((ROWS, D), BF16),
+            pltpu.SemaphoreType.DMA((4,)),
         ],
         prefetch=1,
         vmem=18,
         flops=4 * CENT * ROWS * D,
         nbytes=30 << 20,
-    )(z, dens, freqs, inv, kern, in_hbm(centroids), zn)
-
-
-def hop_body(k, at, a, b, kl, got_right, got_left, right, left):
-    for part, got, msg, first in ((a, got_right, right, 0), (b, got_left, left, HALF)):
-        v, slots = decode(got)
-        full = part[0]
+    )(z, dens, freqs, inv, in_hbm(kern), in_hbm(centroids), zn)
+
+
+PIECES = 4
+
+
+def chunk_loads(z, g, k, part, sems):
+    chunk = lax.rem(z[0] + k + NZ, NZ)
+    rows = [pl.ds(q * (CENT // PIECES), CENT // PIECES) for q in range(PIECES)]
+    return [pltpu.make_async_copy(g.at[chunk, r], part.at[r], sems.at[q]) for q, r in enumerate(rows)]
+
+
+def hop_body(k, z, g, kl, got_right, got_left, right, left, ahead, behind, sems):
+    loads = [chunk_loads(z, g, (k, -k)[i], (ahead, behind)[i], sems.at[i]) for i in range(2)]
+    for cp in loads[0] + loads[1]:
+        cp.start()
+    sums = [decode(got_right), decode(got_left)]
+    for cp in loads[0] + loads[1]:
+        cp.wait()
+    for (v, slots), msg, part, first in zip(sums, (right, left), (ahead, behind), (0, HALF)):
         if k == NZ // 2 - 1:
-            own = full[first : first + HALF, :] + v
-            rest = full[HALF - first : CENT - first, :]
+            own = part[first : first + HALF, :] + v
+            rest = part[HALF - first : CENT - first, :]
             full = jnp.concatenate([own, rest] if first == 0 else [rest, own], axis=0)
         else:
-            full = full + v
+            full = part[...] + v
         encode(full, slots + kl[0:1, :], msg)
-
-
-def part_spec(k):
-    return pl.BlockSpec((1, CENT, CHUNK), lambda s, z: (lax.rem(z[0] + k + NZ, NZ), 0, 0))
 
 
 def hop_call(z, g, kl, k, got):
     return call(
         functools.partial(hop_body, k),
         (1,),
-        [part_spec(k), part_spec(-k), whole((8, LANES)), whole(got[0].shape), whole(got[1].shape)],
+        [pl.BlockSpec(memory_space=pl.ANY), whole((8, LANES)), whole(got[0].shape), whole(got[1].shape)],
         [whole(MSG), whole(MSG)],
         [shaped(MSG, BF16)] * 2,
+        [
+            pltpu.VMEM((CENT, CHUNK), F32),
+            pltpu.VMEM((CENT, CHUNK), F32),
+            pltpu.SemaphoreType.DMA((2, PIECES)),
+        ],
         prefetch=1,
         vmem=14,
         flops=4 * CENT * CHUNK * 40,
         nbytes=3 << 20,
-    )(z, g, g, kl, *got)
-
-
-def end_body(at, own, kl, right, left, out, loss):
+    )(z, in_hbm(g), kl, *got)
+
+
+def end_body(z, g, kl, right, left, out, loss, own, sems):
+    loads = chunk_loads(z, g, 0, own, sems)
+    for cp in loads:
+        cp.start()
     (r, before), (l, after) = decode(right), decode(left)
-    out[...] = (own[0] + r + l) * -SCALE
-    total = jnp.sum(kl[0:1, :] + before + after, axis=1, keepdims=True)
-    loss[...] = jnp.broadcast_to(total, loss.shape)
+    for cp in loads:
+        cp.wait()
+    out[...] = (own[...] + r + l) * -SCALE
+    loss[0, 0] = jnp.sum(kl[0:1, :] + before + after)
 
 
 def end_call(z, g, kl, right, left):
     return call(
         end_body,
         (1,),
-        [part_spec(0), whole((8, LANES)), whole(MSG), whole(MSG)],
-        [whole((CENT, CHUNK)), whole((8, LANES))],
-        [shaped((CENT, CHUNK)), shaped((8, LANES))],
+        [pl.BlockSpec(memory_space=pl.ANY), whole((8, LANES)), whole(MSG), whole(MSG)],
+        [whole((CENT, CHUNK)), pl.BlockSpec(memory_space=pltpu.SMEM)],
+        [shaped((CENT, CHUNK)), shaped((1, 1))],
+        [pltpu.VMEM((CENT, CHUNK), F32), pltpu.SemaphoreType.DMA((PIECES,))],
         prefetch=1,
         vmem=10,
         flops=4 * CENT * CHUNK * 20,
         nbytes=4 << 20,
-    )(z, g, kl, right, left)
-
-
-def point_body(cent, hi, lo, csum, zt, out):
+    )(z, in_hbm(g), kl, right, left)
+
+
+def point_body(cent, hi, lo, csum, zt, *refs):
+    out = refs[-1]
     c = cent[...]
     dims = (((0,), (0,)), ((), ()))
     g = lax.dot_general(c, hi[...], dims, preferred_element_type=F32)
@@ -454,24 +506,29 @@
         out[k, :, ROWS:] = jnp.broadcast_to(expo, (BLOCK, LANES)).astype(BF16)
 
 
-def point_call(centroids, hi, lo, csum, zt):
+def point_call(half, centroids, hi, lo, csum, zt, msgs=None):
     block = (TILE // BLOCK, BLOCK, ROWS + LANES)
-    return call(
+    steps = D // TILE // 2
+    shape = (NCENT, BLOCK, ROWS + LANES)
+    return pl.pallas_call(
         point_body,
-        (D // TILE,),
-        [
-            pl.BlockSpec((CENT, TILE), lambda s: (0, s)),
+        grid=(steps,),
+        in_specs=[
+            pl.BlockSpec((CENT, TILE), lambda s: (0, s + half * steps)),
             whole((CENT, ROWS)),
             whole((CENT, ROWS)),
             whole((8, ROWS)),
-            pl.BlockSpec((TILE, ROWS), lambda s: (s, 0)),
-        ],
-        pl.BlockSpec(block, lambda s: (s, 0, 0)),
-        shaped((NCENT, BLOCK, ROWS + LANES), BF16),
-        vmem=18,
-        flops=4 * CENT * ROWS * D,
-        nbytes=18 << 20,
-    )(in_hbm(centroids), hi, lo, csum, zt)
+            pl.BlockSpec((TILE, ROWS), lambda s: (s + half * steps, 0)),
+        ]
+        + ([] if msgs is None else [pl.BlockSpec(memory_space=pl.ANY)]),
+        out_specs=pl.BlockSpec(block, lambda s: (s + half * steps, 0, 0)),
+        out_shape=pltpu.HBM(shape, BF16),
+        input_output_aliases={} if msgs is None else {5: 0},
+        compiler_params=pltpu.CompilerParams(
+            dimension_semantics=("arbitrary",), vmem_limit_bytes=18 << 20
+        ),
+        cost_estimate=pl.CostEstimate(flops=2 * CENT * ROWS * D, bytes_accessed=9 << 20, transcendentals=0),
+    )(in_hbm(centroids), hi, lo, csum, in_hbm(zt), *([] if msgs is None else [msgs]))
 
 
 def point_sum_body(msgs, out):
@@ -522,16 +579,19 @@
         return lax.ppermute(right, "pts", z_shift(1)), lax.ppermute(left, "pts", z_shift(-1))
 
     got = send(ra, la)
-    msgs = hop_call(z, g, kl, 3, got)
-    hi, lo, right, left = lax.optimization_barrier((hi, lo, *msgs))
+    pmsgs = point_call(0, centroids, hi, lo, csum, zt)
+    pmsgs, right, left = lax.optimization_barrier((pmsgs, *got))
+    msgs = hop_call(z, g, kl, 3, (right, left))
+    pmsgs, right, left = lax.optimization_barrier((pmsgs, *msgs))
     got = send(right, left)
-    pmsgs = point_call(centroids, hi, lo, csum, zt)
+    pmsgs = point_call(1, centroids, hi, lo, csum, zt, pmsgs)
     pmsgs, right, left = lax.optimization_barrier((pmsgs, *got))
-    got = (right, left)
-    for k in (2, 1):
-        got = send(*hop_call(z, g, kl, k, got))
-    grad_centroids, loss = end_call(z, g, kl, *got)
-    grad_points = point_sum_call(lax.all_to_all(pmsgs, "cent", 0, 0)).T
+    got = send(*hop_call(z, g, kl, 2, (right, left)))
+    got = send(*hop_call(z, g, kl, 1, got))
+    points_t = point_sum_call(lax.all_to_all(pmsgs, "cent", 0, 0))
+    points_t, right, left = lax.optimization_barrier((points_t, *got))
+    grad_centroids, loss = end_call(z, g, kl, right, left)
+    grad_points = points_t.T
     return (grad_points, grad_centroids, loss[0, 0])
 
 

time: 188 us -> 182 us (0.968)
  Pallas kernels: 56.7 us -> 67.4 us
  local copies, waits for them, and re-layouts: 11.5 us -> 0.98 us
  waiting for transfers between devices: 52.5 us -> 46.5 us
    ppermute x4, waiting for transfers between devices: 30.1 us -> 19.8 us  [send(): lax.ppermute(right, 'pts', z_shift(1))]
    unnamed x22 -> x6, local copies, waits for them, and re-layouts: 11 us -> 0.98 us
    pallas_call x6 -> x7, Pallas kernels: 34.2 us -> 42 us  [the longest x2 16.2 us: point_call(): pl.pallas_call(point_body, grid=(steps,), in_specs=[pl.BlockSpec((CENT, T...]
    all_to_all x1, waiting for transfers between devices: 0.01 us -> 4.35 us  [per_device(): points_t = point_sum_call(lax.all_to_all(pmsgs, 'cent', 0, 0))]
    pallas_call x1, Pallas kernels: 14.3 us -> 17.1 us  [coef_call(): call(coef_body, (WSTEPS,), [whole((NCENT, 16, LANES)), whole((NZ, CENT //...]
  transfers between devices with their start and end apart: 17 -> 17, of which waited for: 11 -> 12; matrix products, arithmetic and copies ran while one was open for 0% -> 0% of each run, Pallas kernels for 11% -> 14%
where the time goes in v3:
time: 182 us; the launch traced here: 181 us
  Pallas kernels  67.4 us (37%)
  waiting for transfers between devices  46.5 us (26%)
  starting transfers between devices  33.4 us (18%)
  blocking collectives  30.8 us (17%)
    ppermute x4, waiting for transfers between devices, send(): lax.ppermute(right, 'pts', z_shift(1))  19.8 us
    pallas_call x1, Pallas kernels, coef_call(): call(coef_body, (WSTEPS,), [whole((NCENT, 16, LANES)), whole((NZ, CENT //...  17.1 us
    all_to_all x1, blocking collectives, per_device(): freqs = lax.all_to_all(freq, 'pts', 0, 0)  16.6 us
    pallas_call x2, Pallas kernels, point_call(): pl.pallas_call(point_body, grid=(steps,), in_specs=[pl.BlockSpec((CENT, T...  16.2 us
    all_to_all x1, blocking collectives, per_device(): norms = lax.all_to_all(norm, 'cent', 0, 0)  14.2 us
    pallas_call x1, Pallas kernels, kern_call(): call(kern_body, (WSTEPS,), [hbm, hbm, pl.BlockSpec((WIDE, D), lambda s, *...  13.1 us
    ppermute x4, starting transfers between devices, send(): lax.ppermute(left, 'pts', z_shift(-1))  12.5 us
    ppermute x6, waiting for transfers between devices, stage(): lax.ppermute(v, 'cent', cent_shift(*d))  12.4 us
  transfers between devices with their start and end apart: 17, of which 12 were waited for; matrix products, arithmetic and copies ran while one was open for 0% of the time, Pallas kernels for 14%

profile of v3, /device:TPU:8, one launch (start us, length us, event | category | flops | bytes accessed | tf_op | source)
XLA Modules:
  0.0 181.2 jit_solution(5027109684863198049)
XLA Ops:
  0.6 2.4 %collective-permute-start.1 = (bf16[32,1024]{1,0:T(8,128)(2,1)}, bf16[32,1024]{1,0:T(8,128)(2,1)S(1)}, u32[]{:S(2)}, u32[]{:S(2)}) collective-permute-start(bf16[32,1024]{1,0:T(8,128)(2,1)} %bitcast.21), channel_id=1, source_target_pairs={{0,4},{1,5},{2,6},{3,7},{4,0},{5,1},{6,2},{7,3},{8,12},{9,13},{10,... | collective-permute-start | bytes 196616 | tf_op jit(solution)/shard_map/ppermute | solution.py:556
  3.0 1.4 collective-permute-start
  4.4 0.7 collective-permute-start.2
  5.0 1.7 collective-permute-done.1
  6.8 1.0 collective-permute-done
  7.8 1.1 collective-permute-done.2
  8.8 0.9 fusion
  9.7 2.1 %collective-permute-start.4 = (bf16[4,32,1024]{2,1,0:T(8,128)(2,1)S(1)}, bf16[4,32,1024]{2,1,0:T(8,128)(2,1)S(1)}, u32[]{:S(2)}, u32[]{:S(2)}) collective-permute-start(bf16[4,32,1024]{2,1,0:T(8,128)(2,1)S(1)} %get-tuple-element.70), channel_id=1, source_target_pairs={{0,16},{1,17},{2,18},{3,19},{4,20},{5,21},{6,22},{7,23},{8,24},{9,... | collective-permute-start | bytes 786440 | tf_op jit(solution)/shard_map/ppermute | solution.py:556
  11.8 0.6 collective-permute-start.3
  12.4 2.6 %collective-permute-start.5 = (bf16[4,32,1024]{2,1,0:T(8,128)(2,1)S(1)}, bf16[4,32,1024]{2,1,0:T(8,128)(2,1)S(1)}, u32[]{:S(2)}, u32[]{:S(2)}) collective-permute-start(bf16[4,32,1024]{2,1,0:T(8,128)(2,1)S(1)} %get-tuple-element.70), channel_id=1, source_target_pairs={{0,24},{1,25},{2,26},{3,27},{4,28},{5,29},{6,30},{7,31},{8,0},{9,1... | collective-permute-start | bytes 786440 | tf_op jit(solution)/shard_map/ppermute | solution.py:556
  15.0 5.5 %collective-permute-done.4 = bf16[4,32,1024]{2,1,0:T(8,128)(2,1)S(1)} collective-permute-done((bf16[4,32,1024]{2,1,0:T(8,128)(2,1)S(1)}, bf16[4,32,1024]{2,1,0:T(8,128)(2,1)S(1)}, u32[]{:S(2)}, u32[]{:S(2)}) %collective-permute-start.4) | collective-permute-done | bytes 262176 | tf_op jit(solution)/shard_map/ppermute | solution.py:556
  20.5 2.8 %collective-permute-done.3 = bf16[4,32,1024]{2,1,0:T(8,128)(2,1)S(1)} collective-permute-done((bf16[4,32,1024]{2,1,0:T(8,128)(2,1)S(1)}, bf16[4,32,1024]{2,1,0:T(8,128)(2,1)S(1)}, u32[]{:S(2)}, u32[]{:S(2)}) %collective-permute-start.3) | collective-permute-done | bytes 262176 | tf_op jit(solution)/shard_map/ppermute | solution.py:556
  23.3 0.3 collective-permute-done.5
  23.6 0.1 pad_maximum_fusion.mine
  23.7 0.1 collective-permute-start.6
  23.9 0.1 pad_add_fusion.at
  23.9 2.5 %collective-permute-done.6.other = bf16[4,4,32,1024]{3,2,1,0:T(8,128)(2,1)S(1)} collective-permute-done((bf16[4,4,32,1024]{3,2,1,0:T(8,128)(2,1)S(1)}, bf16[4,4,32,1024]{3,2,1,0:T(8,128)(2,1)S(1)}, u32[]{:S(2)}, u32[]{:S(2)}) %collective-permute-start.6) | collective-permute-done | bytes 1048608 | tf_op jit(solution)/shard_map/ppermute | solution.py:560
  26.5 1.0 copy-done.2
  27.4 13.1 %shard_map.49 = (f32[2048,1024]{1,0:T(8,128)S(1)}, f32[32,8,128]{2,1,0:T(8,128)S(1)}, bf16[1024,1024]{1,0:T(8,128)(2,1)}, bf16[1024,1024]{1,0:T(8,128)(2,1)}) custom-call(s32[3]{0:T(128)S(1)} %pad_add_fusion.at, bf16[4,4,32,1024]{3,2,1,0:T(8,128)(2,1)S(1)} %pad_maximum_fusion.mine, bf16[4,4,32,1024]{3,2,1,0:T(8,128)(2,1)} %copy-done.2, bf16[2048,1024]{1,0:T(8,128)(2,1)} %cent.7), custom_call_target="tpu_custom_call" | custom-call | flops 4294967296 | bytes 20971520 | tf_op jit(solution)/shard_map/pallas_call | solution.py:175
  40.6 14.2 %all_to_all.20.norms = f32[32,8,128]{2,1,0:T(8,128)S(1)} all-to-all(f32[32,8,128]{2,1,0:T(8,128)S(1)} %get-tuple-element.36), channel_id=1, replica_groups=mesh['pts'=8,'cent'=32] {'cent'}, dimensions={0} | all-to-all | bytes 262144 | tf_op jit(solution)/shard_map/all_to_all | solution.py:571
  54.8 1.3 shard_map.50
  56.1 16.6 %all_to_all.21.freqs = f32[8,16,128]{2,1,0:T(8,128)S(1)} all-to-all(f32[8,16,128]{2,1,0:T(8,128)S(1)} %get-tuple-element.38), channel_id=1, replica_groups=mesh['pts'=8,'cent'=32] {'pts'}, dimensions={0} | all-to-all | bytes 131072 | tf_op jit(solution)/shard_map/all_to_all | solution.py:573
  72.7 3.9 %shard_map.51 = f32[32,16,128]{2,1,0:T(8,128)} custom-call(f32[8,16,128]{2,1,0:T(8,128)S(1)} %all_to_all.21.freqs, f32[8,128]{1,0:T(8,128)S(1)} %get-tuple-element.39.inv, f32[2048,1024]{1,0:T(8,128)S(1)} %get-tuple-element.37.kern), custom_call_target="tpu_custom_call" | custom-call | flops 12582912 | bytes 8388608 | tf_op jit(solution)/shard_map/pallas_call | solution.py:259
  76.6 5.0 %all-to-all-start.2 = ((f32[32,16,128]{2,1,0:T(8,128)}), f32[32,16,128]{2,1,0:T(8,128)S(1)}, u32[]{:S(2)}, u32[]{:S(2)}) async-start(f32[32,16,128]{2,1,0:T(8,128)} %shard_map.51), calls=%async_computation.2 | async-start | bytes 524288 | tf_op jit(solution)/shard_map/all_to_all | solution.py:575
  81.7 7.4 %all-to-all-done.2.dens = f32[32,16,128]{2,1,0:T(8,128)S(1)} async-done(((f32[32,16,128]{2,1,0:T(8,128)}), f32[32,16,128]{2,1,0:T(8,128)S(1)}, u32[]{:S(2)}, u32[]{:S(2)}) %all-to-all-start.2) | async-done | bytes 262176 | tf_op jit(solution)/shard_map/all_to_all | solution.py:575
  89.1 17.1 %shard_map.52 = (bf16[2048,1024]{1,0:T(8,128)(2,1)S(1)}, bf16[2048,1024]{1,0:T(8,128)(2,1)S(1)}, f32[8,1024]{1,0:T(8,128)S(1)}, f32[8,128]{1,0:T(8,128)S(1)}, f3...) custom-call(s32[1]{0:T(128)} %bitcast.z, ...), custom_call_target="tpu_custom_call" | custom-call | flops 8589934592 | bytes 31457280 | tf_op jit(solution)/shard_map/pallas_call | solution.py:380
  106.2 0.6 collective-permute-start.7
  106.9 2.7 %collective-permute-start.8 = (bf16[1040,128]{1,0:T(8,128)(2,1)S(1)}, bf16[1040,128]{1,0:T(8,128)(2,1)S(1)}, u32[]{:S(2)}, u32[]{:S(2)}) collective-permute-start(bf16[1040,128]{1,0:T(8,128)(2,1)S(1)} %get-tuple-element.46), channel_id=1, source_target_pairs={{0,224},{32,0},{64,32},{96,64},{128,96},{160,128},{192,160},{224,1... | collective-permute-start | bytes 798728 | tf_op jit(solution)/shard_map/ppermute | solution.py:579
  109.6 8.1 %shard_map.53.refs_0_ = bf16[32,32,1152]{2,1,0:T(8,128)(2,1)} custom-call(bf16[2048,1024]{1,0:T(8,128)(2,1)} %cent.7, bf16[2048,1024]{1,0:T(8,128)(2,1)S(1)} %get-tuple-element.41.hi, bf16[2048,1024]{1,0:T(8,128)(2,1)S(1)} %get-tuple-element.42.lo, f32[8,1024]{1,0:T(8,128)S(1)} %get-tuple-element.43.csum, bf16[1024,1024]{1,0:T(8,128)(2,1)} %get-tuple-element.44.zt), custom_call_target="tpu_custom_call" | custom-call | flops 4294967296 | bytes 9437184 | tf_op jit(solution)/shard_map/pallas_call | solution.py:513
  117.6 0.0 collective-permute-done.7.got_right
  117.6 3.1 %shard_map.54 = (bf16[2064,128]{1,0:T(8,128)(2,1)S(1)}, bf16[2064,128]{1,0:T(8,128)(2,1)S(1)}) custom-call(s32[1]{0:T(128)} %bitcast.z, f32[8,2048,128]{2,1,0:T(8,128)} %get-tuple-element.48.g, f32[8,128]{1,0:T(8,128)S(1)} %get-tuple-element.49.kl, bf16[1040,128]{1,0:T(8,128)(2,1)S(1)} %collective-permute-done.7.got_right, ...), custom_call_target="tpu_custom_call" | custom-call | flops 41943040 | bytes 3145728 | tf_op jit(solution)/shard_map/pallas_call | solution.py:451
  120.7 0.1 collective-permute-start.9
  120.8 3.2 %collective-permute-start.10 = (bf16[2064,128]{1,0:T(8,128)(2,1)S(1)}, bf16[2064,128]{1,0:T(8,128)(2,1)S(1)}, u32[]{:S(2)}, u32[]{:S(2)}) collective-permute-start(bf16[2064,128]{1,0:T(8,128)(2,1)S(1)} %get-tuple-element.56), channel_id=1, source_target_pairs={{0,224},{32,0},{64,32},{96,64},{128,96},{160,128},{192,160},{224,1... | collective-permute-start | bytes 1585160 | tf_op jit(solution)/shard_map/ppermute | solution.py:579
  124.0 8.1 %shard_map.55 = bf16[32,32,1152]{2,1,0:T(8,128)(2,1)} custom-call(bf16[2048,1024]{1,0:T(8,128)(2,1)} %cent.7, bf16[2048,1024]{1,0:T(8,128)(2,1)S(1)} %get-tuple-element.41.hi, bf16[2048,1024]{1,0:T(8,128)(2,1)S(1)} %get-tuple-element.42.lo, f32[8,1024]{1,0:T(8,128)S(1)} %get-tuple-element.43.csum, ...), custom_call_target="tpu_custom_call", output_to_operand_aliasing={{}: (5, {})} | custom-call | flops 4294967296 | bytes 9437184 | tf_op jit(solution)/shard_map/pallas_call | solution.py:513
  132.1 3.9 %collective-permute-done.9.got_right = bf16[2064,128]{1,0:T(8,128)(2,1)S(1)} collective-permute-done((bf16[2064,128]{1,0:T(8,128)(2,1)S(1)}, bf16[2064,128]{1,0:T(8,128)(2,1)S(1)}, u32[]{:S(2)}, u32[]{:S(2)}) %collective-permute-start.9) | collective-permute-done | bytes 528416 | tf_op jit(solution)/shard_map/ppermute | solution.py:579
  136.0 0.0 collective-permute-done.10.got_left
  136.0 5.2 %all-to-all-start.3 = ((bf16[32,32,1152]{2,1,0:T(8,128)(2,1)}), bf16[32,32,1152]{2,1,0:T(8,128)(2,1)S(1)}, u32[]{:S(2)}, u32[]{:S(2)}) async-start(bf16[32,32,1152]{2,1,0:T(8,128)(2,1)} %shard_map.55), calls=%async_computation.3 | async-start | bytes 4718592 | tf_op jit(solution)/shard_map/all_to_all | solution.py:591
  141.2 3.1 %shard_map.57 = (bf16[2064,128]{1,0:T(8,128)(2,1)S(1)}, bf16[2064,128]{1,0:T(8,128)(2,1)S(1)}) custom-call(s32[1]{0:T(128)} %bitcast.z, f32[8,2048,128]{2,1,0:T(8,128)} %get-tuple-element.48.g, f32[8,128]{1,0:T(8,128)S(1)} %get-tuple-element.49.kl, bf16[2064,128]{1,0:T(8,128)(2,1)S(1)} %collective-permute-done.9.got_right, ...), custom_call_target="tpu_custom_call" | custom-call | flops 41943040 | bytes 3145728 | tf_op jit(solution)/shard_map/pallas_call | solution.py:451
  144.4 0.1 collective-permute-start.11
  144.4 3.2 %collective-permute-start.12 = (bf16[2064,128]{1,0:T(8,128)(2,1)S(1)}, bf16[2064,128]{1,0:T(8,128)(2,1)S(1)}, u32[]{:S(2)}, u32[]{:S(2)}) collective-permute-start(bf16[2064,128]{1,0:T(8,128)(2,1)S(1)} %get-tuple-element.61), channel_id=1, source_target_pairs={{0,224},{32,0},{64,32},{96,64},{128,96},{160,128},{192,160},{224,1... | collective-permute-start | bytes 1585160 | tf_op jit(solution)/shard_map/ppermute | solution.py:579
  147.7 12.0 %collective-permute-done.11.got_right = bf16[2064,128]{1,0:T(8,128)(2,1)S(1)} collective-permute-done((bf16[2064,128]{1,0:T(8,128)(2,1)S(1)}, bf16[2064,128]{1,0:T(8,128)(2,1)S(1)}, u32[]{:S(2)}, u32[]{:S(2)}) %collective-permute-start.11) | collective-permute-done | bytes 528416 | tf_op jit(solution)/shard_map/ppermute | solution.py:579
  159.7 3.9 %shard_map.58 = (bf16[2064,128]{1,0:T(8,128)(2,1)}, bf16[2064,128]{1,0:T(8,128)(2,1)}) custom-call(s32[1]{0:T(128)} %bitcast.z, f32[8,2048,128]{2,1,0:T(8,128)} %get-tuple-element.48.g, f32[8,128]{1,0:T(8,128)S(1)} %get-tuple-element.49.kl, bf16[2064,128]{1,0:T(8,128)(2,1)S(1)} %collective-permute-done.11.got_right, ...), custom_call_target="tpu_custom_call" | custom-call | flops 41943040 | bytes 3145728 | tf_op jit(solution)/shard_map/pallas_call | solution.py:451
  163.6 0.1 collective-permute-start.13
  163.7 3.4 %collective-permute-start.14 = (bf16[2064,128]{1,0:T(8,128)(2,1)}, bf16[2064,128]{1,0:T(8,128)(2,1)S(1)}, u32[]{:S(2)}, u32[]{:S(2)}) collective-permute-start(bf16[2064,128]{1,0:T(8,128)(2,1)} %get-tuple-element.63), channel_id=1, source_target_pairs={{0,224},{32,0},{64,32},{96,64},{128,96},{160,128},{192,160},{224,1... | collective-permute-start | bytes 1585160 | tf_op jit(solution)/shard_map/ppermute | solution.py:579
  167.1 4.3 %all-to-all-done.3.msgs = bf16[32,32,1152]{2,1,0:T(8,128)(2,1)S(1)} async-done(((bf16[32,32,1152]{2,1,0:T(8,128)(2,1)}), bf16[32,32,1152]{2,1,0:T(8,128)(2,1)S(1)}, u32[]{:S(2)}, u32[]{:S(2)}) %all-to-all-start.3) | async-done | bytes 2359328 | tf_op jit(solution)/shard_map/all_to_all | solution.py:591
  171.4 3.0 %shard_map.56 = f32[32,1024]{1,0:T(8,128)} custom-call(bf16[32,32,1152]{2,1,0:T(8,128)(2,1)S(1)} %all-to-all-done.3.msgs), custom_call_target="tpu_custom_call" | custom-call | flops 20971520 | bytes 3145728 | tf_op jit(solution)/shard_map/pallas_call | solution.py:542
  174.5 3.9 %collective-permute-done.13.right = bf16[2064,128]{1,0:T(8,128)(2,1)S(1)} collective-permute-done((bf16[2064,128]{1,0:T(8,128)(2,1)}, bf16[2064,128]{1,0:T(8,128)(2,1)S(1)}, u32[]{:S(2)}, u32[]{:S(2)}) %collective-permute-start.13) | collective-permute-done | bytes 528416 | tf_op jit(solution)/shard_map/ppermute | solution.py:579
  178.4 2.6 %shard_map.59 = (f32[2048,128]{1,0:T(8,128)}, f32[1,1]{1,0:T(1,128)}) custom-call(s32[1]{0:T(128)} %bitcast.z, f32[8,2048,128]{2,1,0:T(8,128)} %get-tuple-element.48.g, f32[8,128]{1,0:T(8,128)S(1)} %get-tuple-element.49.kl, bf16[2064,128]{1,0:T(8,128)(2,1)S(1)} %collective-permute-done.13.right, bf16[2064,128]{1,0:T(8,128)(2,1)S(1)} %collective-permute-done.14.left), custom_call_target="tpu_custom_call" | custom-call | flops 20971520 | bytes 4194304 | tf_op jit(solution)/shard_map/pallas_call | solution.py:481
  (8 shorter events, 0.0 us)
Async XLA Ops:
  0.6 6.1 %collective-permute-start.1 = (bf16[32,1024]{1,0:T(8,128)(2,1)}, bf16[32,1024]{1,0:T(8,128)(2,1)S(1)}, u32[]{:S(2)}, u32[]{:S(2)}) collective-permute-start(bf16[32,1024]{1,0:T(8,128)(2,1)} %bitcast.21), channel_id=1, source_target_pairs={{0,4},{1,5},{2,6},{3,7},{4,0},{5,1},{6,2},{7,3},{8,12},{9,13},{10,... | collective-permute-start | bytes 196616 | tf_op jit(solution)/shard_map/ppermute | solution.py:556
  3.0 4.8 %collective-permute-start = (bf16[32,1024]{1,0:T(8,128)(2,1)}, bf16[32,1024]{1,0:T(8,128)(2,1)S(1)}, u32[]{:S(2)}, u32[]{:S(2)}) collective-permute-start(bf16[32,1024]{1,0:T(8,128)(2,1)} %bitcast.22), channel_id=1, source_target_pairs={{0,2},{1,3},{2,4},{3,5},{4,6},{5,7},{6,0},{7,1},{8,10},{9,11},{10,... | collective-permute-start | bytes 196616 | tf_op jit(solution)/shard_map/ppermute | solution.py:556
  4.4 4.5 %collective-permute-start.2 = (bf16[32,1024]{1,0:T(8,128)(2,1)}, bf16[32,1024]{1,0:T(8,128)(2,1)S(1)}, u32[]{:S(2)}, u32[]{:S(2)}) collective-permute-start(bf16[32,1024]{1,0:T(8,128)(2,1)} %bitcast.23), channel_id=1, source_target_pairs={{0,6},{1,7},{2,0},{3,1},{4,2},{5,3},{6,4},{7,5},{8,14},{9,15},{10,... | collective-permute-start | bytes 196616 | tf_op jit(solution)/shard_map/ppermute | solution.py:556
  9.7 10.8 %collective-permute-start.4 = (bf16[4,32,1024]{2,1,0:T(8,128)(2,1)S(1)}, bf16[4,32,1024]{2,1,0:T(8,128)(2,1)S(1)}, u32[]{:S(2)}, u32[]{:S(2)}) collective-permute-start(bf16[4,32,1024]{2,1,0:T(8,128)(2,1)S(1)} %get-tuple-element.70), channel_id=1, source_target_pairs={{0,16},{1,17},{2,18},{3,19},{4,20},{5,21},{6,22},{7,23},{8,24},{9,... | collective-permute-start | bytes 786440 | tf_op jit(solution)/shard_map/ppermute | solution.py:556
  11.8 11.5 %collective-permute-start.3 = (bf16[4,32,1024]{2,1,0:T(8,128)(2,1)S(1)}, bf16[4,32,1024]{2,1,0:T(8,128)(2,1)S(1)}, u32[]{:S(2)}, u32[]{:S(2)}) collective-permute-start(bf16[4,32,1024]{2,1,0:T(8,128)(2,1)S(1)} %get-tuple-element.70), channel_id=1, source_target_pairs={{0,8},{1,9},{2,10},{3,11},{4,12},{5,13},{6,14},{7,15},{8,16},{9,17... | collective-permute-start | bytes 786440 | tf_op jit(solution)/shard_map/ppermute | solution.py:556
  12.4 11.2 %collective-permute-start.5 = (bf16[4,32,1024]{2,1,0:T(8,128)(2,1)S(1)}, bf16[4,32,1024]{2,1,0:T(8,128)(2,1)S(1)}, u32[]{:S(2)}, u32[]{:S(2)}) collective-permute-start(bf16[4,32,1024]{2,1,0:T(8,128)(2,1)S(1)} %get-tuple-element.70), channel_id=1, source_target_pairs={{0,24},{1,25},{2,26},{3,27},{4,28},{5,29},{6,30},{7,31},{8,0},{9,1... | collective-permute-start | bytes 786440 | tf_op jit(solution)/shard_map/ppermute | solution.py:556
  23.7 2.7 %collective-permute-start.6 = (bf16[4,4,32,1024]{3,2,1,0:T(8,128)(2,1)S(1)}, bf16[4,4,32,1024]{3,2,1,0:T(8,128)(2,1)S(1)}, u32[]{:S(2)}, u32[]{:S(2)}) collective-permute-start(bf16[4,4,32,1024]{3,2,1,0:T(8,128)(2,1)S(1)} %pad_maximum_fusion.mine), channel_id=1, source_target_pairs={{0,1},{1,0},{2,3},{3,2},{4,5},{5,4},{6,7},{7,6},{8,9},{9,8},{10,11... | collective-permute-start | bytes 3145736 | tf_op jit(solution)/shard_map/ppermute | solution.py:560
  26.5 1.0 copy-start.2
  40.6 32.1 %copy-start = (f32[2048,1024]{1,0:T(8,128)}, f32[2048,1024]{1,0:T(8,128)S(1)}, u32[]{:S(2)}) copy-start(f32[2048,1024]{1,0:T(8,128)S(1)} %get-tuple-element.37.kern) | copy-start | bytes 25165828
  72.7 16.4 %copy-start.1 = (bf16[1024,1024]{1,0:T(8,128)(2,1)S(1)}, bf16[1024,1024]{1,0:T(8,128)(2,1)}, u32[]{:S(2)}) copy-start(bf16[1024,1024]{1,0:T(8,128)(2,1)} %get-tuple-element.40.zn_hbm) | copy-start | bytes 6291460
  76.6 12.5 %all-to-all-start.2 = ((f32[32,16,128]{2,1,0:T(8,128)}), f32[32,16,128]{2,1,0:T(8,128)S(1)}, u32[]{:S(2)}, u32[]{:S(2)}) async-start(f32[32,16,128]{2,1,0:T(8,128)} %shard_map.51), calls=%async_computation.2 | async-start | bytes 524288 | tf_op jit(solution)/shard_map/all_to_all | solution.py:575
  106.2 11.4 %collective-permute-start.7 = (bf16[1040,128]{1,0:T(8,128)(2,1)S(1)}, bf16[1040,128]{1,0:T(8,128)(2,1)S(1)}, u32[]{:S(2)}, u32[]{:S(2)}) collective-permute-start(bf16[1040,128]{1,0:T(8,128)(2,1)S(1)} %get-tuple-element.45), channel_id=1, source_target_pairs={{0,32},{32,64},{64,96},{96,128},{128,160},{160,192},{192,224},{224... | collective-permute-start | bytes 798728 | tf_op jit(solution)/shard_map/ppermute | solution.py:579
  106.9 10.7 %collective-permute-start.8 = (bf16[1040,128]{1,0:T(8,128)(2,1)S(1)}, bf16[1040,128]{1,0:T(8,128)(2,1)S(1)}, u32[]{:S(2)}, u32[]{:S(2)}) collective-permute-start(bf16[1040,128]{1,0:T(8,128)(2,1)S(1)} %get-tuple-element.46), channel_id=1, source_target_pairs={{0,224},{32,0},{64,32},{96,64},{128,96},{160,128},{192,160},{224,1... | collective-permute-start | bytes 798728 | tf_op jit(solution)/shard_map/ppermute | solution.py:579
  120.7 15.3 %collective-permute-start.9 = (bf16[2064,128]{1,0:T(8,128)(2,1)S(1)}, bf16[2064,128]{1,0:T(8,128)(2,1)S(1)}, u32[]{:S(2)}, u32[]{:S(2)}) collective-permute-start(bf16[2064,128]{1,0:T(8,128)(2,1)S(1)} %get-tuple-element.55), channel_id=1, source_target_pairs={{0,32},{32,64},{64,96},{96,128},{128,160},{160,192},{192,224},{224... | collective-permute-start | bytes 1585160 | tf_op jit(solution)/shard_map/ppermute | solution.py:579
  120.8 15.2 %collective-permute-start.10 = (bf16[2064,128]{1,0:T(8,128)(2,1)S(1)}, bf16[2064,128]{1,0:T(8,128)(2,1)S(1)}, u32[]{:S(2)}, u32[]{:S(2)}) collective-permute-start(bf16[2064,128]{1,0:T(8,128)(2,1)S(1)} %get-tuple-element.56), channel_id=1, source_target_pairs={{0,224},{32,0},{64,32},{96,64},{128,96},{160,128},{192,160},{224,1... | collective-permute-start | bytes 1585160 | tf_op jit(solution)/shard_map/ppermute | solution.py:579
  136.0 35.4 %all-to-all-start.3 = ((bf16[32,32,1152]{2,1,0:T(8,128)(2,1)}), bf16[32,32,1152]{2,1,0:T(8,128)(2,1)S(1)}, u32[]{:S(2)}, u32[]{:S(2)}) async-start(bf16[32,32,1152]{2,1,0:T(8,128)(2,1)} %shard_map.55), calls=%async_computation.3 | async-start | bytes 4718592 | tf_op jit(solution)/shard_map/all_to_all | solution.py:591
  144.4 15.4 %collective-permute-start.11 = (bf16[2064,128]{1,0:T(8,128)(2,1)S(1)}, bf16[2064,128]{1,0:T(8,128)(2,1)S(1)}, u32[]{:S(2)}, u32[]{:S(2)}) collective-permute-start(bf16[2064,128]{1,0:T(8,128)(2,1)S(1)} %get-tuple-element.60), channel_id=1, source_target_pairs={{0,32},{32,64},{64,96},{96,128},{128,160},{160,192},{192,224},{224... | collective-permute-start | bytes 1585160 | tf_op jit(solution)/shard_map/ppermute | solution.py:579
  144.4 15.3 %collective-permute-start.12 = (bf16[2064,128]{1,0:T(8,128)(2,1)S(1)}, bf16[2064,128]{1,0:T(8,128)(2,1)S(1)}, u32[]{:S(2)}, u32[]{:S(2)}) collective-permute-start(bf16[2064,128]{1,0:T(8,128)(2,1)S(1)} %get-tuple-element.61), channel_id=1, source_target_pairs={{0,224},{32,0},{64,32},{96,64},{128,96},{160,128},{192,160},{224,1... | collective-permute-start | bytes 1585160 | tf_op jit(solution)/shard_map/ppermute | solution.py:579
  163.6 14.7 %collective-permute-start.13 = (bf16[2064,128]{1,0:T(8,128)(2,1)}, bf16[2064,128]{1,0:T(8,128)(2,1)S(1)}, u32[]{:S(2)}, u32[]{:S(2)}) collective-permute-start(bf16[2064,128]{1,0:T(8,128)(2,1)} %get-tuple-element.62), channel_id=1, source_target_pairs={{0,32},{32,64},{64,96},{96,128},{128,160},{160,192},{192,224},{224... | collective-permute-start | bytes 1585160 | tf_op jit(solution)/shard_map/ppermute | solution.py:579
  163.7 14.6 %collective-permute-start.14 = (bf16[2064,128]{1,0:T(8,128)(2,1)}, bf16[2064,128]{1,0:T(8,128)(2,1)S(1)}, u32[]{:S(2)}, u32[]{:S(2)}) collective-permute-start(bf16[2064,128]{1,0:T(8,128)(2,1)} %get-tuple-element.63), channel_id=1, source_target_pairs={{0,224},{32,0},{64,32},{96,64},{128,96},{160,128},{192,160},{224,1... | collective-permute-start | bytes 1585160 | tf_op jit(solution)/shard_map/ppermute | solution.py:579

commit v4 on v3

--- a/solution.py
+++ b/solution.py
@@ -112,16 +112,9 @@
     for cr in range(NC):
         src = (mine, other)[cr]
         for xr in range(NX):
-            for yr in range(NY):
-                xx = lax.rem(at[0] + NX - xr, NX)
-                yy = lax.rem(at[1] + NY - yr, NY)
-                cc = lax.rem(at[2] + cr, NC)
-                row = pl.multiple_of(((xx * NY + yy) * NC + cc) * BLOCK, BLOCK)
-                copies.append(
-                    pltpu.make_async_copy(
-                        src.at[xr, yr], zt.at[pl.ds(row, BLOCK), :], sems.at[(cr * NX + xr) * NY + yr]
-                    )
-                )
+            xx = lax.rem(at[0] + NX - xr, NX)
+            cc = lax.rem(at[2] + cr, NC)
+            copies.append(pltpu.make_async_copy(src.at[xr], zt.at[xx, :, cc], sems.at[cr * NX + xr]))
 
     @pl.when(step == 0)
     def _():
@@ -144,7 +137,8 @@
         outs[0].start()
         total = jnp.zeros((8, ROWS), F32)
         for k in range(D // LANES):
-            v = zt[k * LANES : (k + 1) * LANES, :].astype(F32)
+            pair = slice(k % 2 * 2, k % 2 * 2 + 2)
+            v = zt[k // 2, pair].reshape(LANES, ROWS).astype(F32)
             v = v * v
             total = total + jnp.sum(v.reshape(LANES // 8, 8, ROWS), axis=0)
         zsq[...] = 1.0 + jnp.sum(total, axis=0, keepdims=True)
@@ -152,7 +146,7 @@
 
     for k in range(ROWS // SLAB):
         cols = slice(k * SLAB, (k + 1) * SLAB)
-        dots = dot(c, zt[:, cols])
+        dots = dot(c, zt[:, :, :, :, cols].reshape(D, SLAB))
         v = 1.0 / ((zsq[:, cols] + msq) - 2.0 * dots)
         kern[:, cols] = v
         acc[:, cols] += jnp.sum(v.reshape(WIDE // 8, 8, SLAB), axis=0)
@@ -160,7 +154,7 @@
 
         @pl.when(step == t)
         def _(t=t):
-            zn[:, t * part : (t + 1) * part] = jnp.transpose(zt[t * part : (t + 1) * part, :])
+            zn[:, t * part : (t + 1) * part] = jnp.transpose(zt[t].reshape(part, ROWS))
             outs[1 + t].start()
 
     @pl.when(step == WSTEPS - 1)
@@ -180,22 +174,22 @@
         [
             shaped((CENT, ROWS)),
             shaped((NCENT, 8, LANES)),
-            pltpu.HBM((D, ROWS), BF16),
+            pltpu.HBM((NX, NY, NC, BLOCK, ROWS), BF16),
             pltpu.HBM((ROWS, D), BF16),
         ],
         [
-            pltpu.VMEM((D, ROWS), BF16),
+            pltpu.VMEM((NX, NY, NC, BLOCK, ROWS), BF16),
             pltpu.VMEM((ROWS, D), BF16),
             pltpu.VMEM((1, ROWS), F32),
             pltpu.VMEM((8, ROWS), F32),
-            pltpu.SemaphoreType.DMA((NCENT,)),
+            pltpu.SemaphoreType.DMA((NC * NX,)),
             pltpu.SemaphoreType.DMA((WSTEPS + 1,)),
         ],
         prefetch=1,
         vmem=18,
         flops=2 * CENT * ROWS * D,
         nbytes=20 << 20,
-    )(at, mine, in_hbm(other), in_hbm(centroids))
+    )(at, mine, other, in_hbm(centroids))
 
 
 def freq_body(norms, kern, freq, inv, row):
@@ -506,28 +500,27 @@
         out[k, :, ROWS:] = jnp.broadcast_to(expo, (BLOCK, LANES)).astype(BF16)
 
 
-def point_call(half, centroids, hi, lo, csum, zt, msgs=None):
+def point_call(first, steps, centroids, hi, lo, csum, zt, msgs=None):
     block = (TILE // BLOCK, BLOCK, ROWS + LANES)
-    steps = D // TILE // 2
     shape = (NCENT, BLOCK, ROWS + LANES)
     return pl.pallas_call(
         point_body,
         grid=(steps,),
         in_specs=[
-            pl.BlockSpec((CENT, TILE), lambda s: (0, s + half * steps)),
+            pl.BlockSpec((CENT, TILE), lambda s: (0, s + first)),
             whole((CENT, ROWS)),
             whole((CENT, ROWS)),
             whole((8, ROWS)),
-            pl.BlockSpec((TILE, ROWS), lambda s: (s + half * steps, 0)),
+            pl.BlockSpec((TILE, ROWS), lambda s: (s + first, 0)),
         ]
         + ([] if msgs is None else [pl.BlockSpec(memory_space=pl.ANY)]),
-        out_specs=pl.BlockSpec(block, lambda s: (s + half * steps, 0, 0)),
+        out_specs=pl.BlockSpec(block, lambda s: (s + first, 0, 0)),
         out_shape=pltpu.HBM(shape, BF16),
         input_output_aliases={} if msgs is None else {5: 0},
         compiler_params=pltpu.CompilerParams(
             dimension_semantics=("arbitrary",), vmem_limit_bytes=18 << 20
         ),
-        cost_estimate=pl.CostEstimate(flops=2 * CENT * ROWS * D, bytes_accessed=9 << 20, transcendentals=0),
+        cost_estimate=pl.CostEstimate(flops=CENT * ROWS * D * steps, bytes_accessed=9 << 20, transcendentals=0),
     )(in_hbm(centroids), hi, lo, csum, in_hbm(zt), *([] if msgs is None else [msgs]))
 
 
@@ -551,12 +544,30 @@
     )(msgs)
 
 
-def gather_points(v):
+def order_body(at, *refs):
+    for k in range(NY):
+        refs[-1][pl.ds(lax.rem(at[1] + NY - k, NY), 1)] = refs[k][...][None]
+
+
+def order_call(at, blocks):
+    return call(
+        order_body,
+        (1,),
+        [whole((BLOCK, ROWS))] * NY,
+        whole((NY, BLOCK, ROWS)),
+        shaped((NY, BLOCK, ROWS), BF16),
+        prefetch=1,
+        nbytes=1 << 19,
+    )(at, *blocks)
+
+
+def gather_points(at, v):
     def stage(v, shifts):
-        return jnp.stack([v] + [lax.ppermute(v, "cent", cent_shift(*d)) for d in shifts])
-
-    v = stage(v, [(0, k, 0) for k in (1, 2, 3)])
-    v = stage(v, [(k, 0, 0) for k in (1, 2, 3)])
+        return [v] + [lax.ppermute(v, "cent", cent_shift(*d)) for d in shifts]
+
+    v = order_call(at, stage(v, [(0, k, 0) for k in (1, 2, 3)]))
+    v0, v1, v3, v2 = stage(v, [(k, 0, 0) for k in (1, 3, 2)])
+    v = jnp.stack([v0, v1, v2, v3])
     return v, lax.ppermute(v, "cent", cent_shift(0, 0, 1))
 
 
@@ -566,8 +577,9 @@
     at = jnp.stack([x, y, c]).astype(jnp.int32)
     zi = lax.axis_index("pts").astype(jnp.int32)
     z = zi[None]
-    mine, other = gather_points(points.T)
+    mine, other = gather_points(at, points.T)
     kern, norm, zt, zn = kern_call(at, mine, other, centroids)
+    zt = zt.reshape(D, ROWS)
     norms = lax.all_to_all(norm, "cent", 0, 0)
     freq, inv = freq_call(norms, kern)
     freqs = lax.all_to_all(freq, "pts", 0, 0)
@@ -579,12 +591,12 @@
         return lax.ppermute(right, "pts", z_shift(1)), lax.ppermute(left, "pts", z_shift(-1))
 
     got = send(ra, la)
-    pmsgs = point_call(0, centroids, hi, lo, csum, zt)
+    pmsgs = point_call(0, 1, centroids, hi, lo, csum, zt)
     pmsgs, right, left = lax.optimization_barrier((pmsgs, *got))
     msgs = hop_call(z, g, kl, 3, (right, left))
     pmsgs, right, left = lax.optimization_barrier((pmsgs, *msgs))
     got = send(right, left)
-    pmsgs = point_call(1, centroids, hi, lo, csum, zt, pmsgs)
+    pmsgs = point_call(1, D // TILE - 1, centroids, hi, lo, csum, zt, pmsgs)
     pmsgs, right, left = lax.optimization_barrier((pmsgs, *got))
     got = send(*hop_call(z, g, kl, 2, (right, left)))
     got = send(*hop_call(z, g, kl, 1, got))

time: 182 us -> 177 us (0.973)
  Pallas kernels: 67.4 us -> 65.3 us
  blocking collectives: 30.8 us -> 28.8 us
    ppermute x6, waiting for transfers between devices: 12.4 us -> 15.2 us  [stage(): return [v] + [lax.ppermute(v, 'cent', cent_shift(*d)) for d in shifts]]
    pallas_call x1, Pallas kernels: 13.1 us -> 10.3 us  [kern_call(): call(kern_body, (WSTEPS,), [hbm, hbm, pl.BlockSpec((WIDE, D), lambda s, *...]
    all_to_all x1, blocking collectives: 14.2 us -> 12.2 us  [per_device(): norms = lax.all_to_all(norm, 'cent', 0, 0)]
  transfers between devices with their start and end apart: 17 -> 17, of which waited for: 12 -> 11; matrix products, arithmetic and copies ran while one was open for 0% -> 0% of each run, Pallas kernels for 14% -> 15%
where the time goes in v4:
time: 177 us; the launch traced here: 176 us
  Pallas kernels  65.3 us (37%)
  waiting for transfers between devices  47.9 us (27%)
  starting transfers between devices  32.3 us (18%)
  blocking collectives  28.8 us (16%)
    ppermute x4, waiting for transfers between devices, send(): lax.ppermute(right, 'pts', z_shift(1))  18.2 us
    pallas_call x1, Pallas kernels, coef_call(): call(coef_body, (WSTEPS,), [whole((NCENT, 16, LANES)), whole((NZ, CENT //...  17.1 us
    all_to_all x1, blocking collectives, per_device(): freqs = lax.all_to_all(freq, 'pts', 0, 0)  16.6 us
    pallas_call x2, Pallas kernels, point_call(): pl.pallas_call(point_body, grid=(steps,), in_specs=[pl.BlockSpec((CENT, T...  16.3 us
    ppermute x6, waiting for transfers between devices, stage(): return [v] + [lax.ppermute(v, 'cent', cent_shift(*d)) for d in shifts]  15.2 us
    ppermute x4, starting transfers between devices, send(): lax.ppermute(left, 'pts', z_shift(-1))  12.5 us
    all_to_all x1, blocking collectives, per_device(): norms = lax.all_to_all(norm, 'cent', 0, 0)  12.2 us
    pallas_call x1, Pallas kernels, kern_call(): call(kern_body, (WSTEPS,), [hbm, hbm, pl.BlockSpec((WIDE, D), lambda s, *...  10.3 us
  transfers between devices with their start and end apart: 17, of which 11 were waited for; matrix products, arithmetic and copies ran while one was open for 0% of the time, Pallas kernels for 15%

profile of v4, /device:TPU:8, one launch (start us, length us, event | category | flops | bytes accessed | tf_op | source)
XLA Modules:
  0.0 176.4 jit_solution(949382286988648377)
XLA Ops:
  0.6 2.3 %collective-permute-start.2 = (bf16[32,1024]{1,0:T(8,128)(2,1)}, bf16[32,1024]{1,0:T(8,128)(2,1)S(1)}, u32[]{:S(2)}, u32[]{:S(2)}) collective-permute-start(bf16[32,1024]{1,0:T(8,128)(2,1)} %bitcast.13), channel_id=1, source_target_pairs={{0,6},{1,7},{2,0},{3,1},{4,2},{5,3},{6,4},{7,5},{8,14},{9,15},{10,... | collective-permute-start | bytes 196616 | tf_op jit(solution)/shard_map/ppermute | solution.py:566
  2.9 0.9 collective-permute-start.1
  3.7 1.9 %collective-permute-start = (bf16[32,1024]{1,0:T(8,128)(2,1)}, bf16[32,1024]{1,0:T(8,128)(2,1)S(1)}, u32[]{:S(2)}, u32[]{:S(2)}) collective-permute-start(bf16[32,1024]{1,0:T(8,128)(2,1)} %bitcast.15), channel_id=1, source_target_pairs={{0,2},{1,3},{2,4},{3,5},{4,6},{5,7},{6,0},{7,1},{8,10},{9,11},{10,... | collective-permute-start | bytes 196616 | tf_op jit(solution)/shard_map/ppermute | solution.py:566
  5.6 0.1 pad_add_fusion.at
  5.7 0.0 collective-permute-done.2.refs_3_
  5.7 3.1 %collective-permute-done.1.refs_2_ = bf16[32,1024]{1,0:T(8,128)(2,1)S(1)} collective-permute-done((bf16[32,1024]{1,0:T(8,128)(2,1)}, bf16[32,1024]{1,0:T(8,128)(2,1)S(1)}, u32[]{:S(2)}, u32[]{:S(2)}) %collective-permute-start.1) | collective-permute-done | bytes 65568 | tf_op jit(solution)/shard_map/ppermute | solution.py:566
  8.9 0.0 collective-permute-done.refs_1_
  8.9 0.8 copy-done.1
  9.7 0.6 shard_map.49
  10.3 2.2 %collective-permute-start.5 = (bf16[4,32,1024]{2,1,0:T(8,128)(2,1)S(1)}, bf16[4,32,1024]{2,1,0:T(8,128)(2,1)S(1)}, u32[]{:S(2)}, u32[]{:S(2)}) collective-permute-start(bf16[4,32,1024]{2,1,0:T(8,128)(2,1)S(1)} %shard_map.49), channel_id=1, source_target_pairs={{0,24},{1,25},{2,26},{3,27},{4,28},{5,29},{6,30},{7,31},{8,0},{9,1... | collective-permute-start | bytes 786440 | tf_op jit(solution)/shard_map/ppermute | solution.py:566
  12.5 0.8 collective-permute-start.4
  13.3 0.9 collective-permute-start.3
  14.2 8.3 %collective-permute-done.5 = bf16[4,32,1024]{2,1,0:T(8,128)(2,1)S(1)} collective-permute-done((bf16[4,32,1024]{2,1,0:T(8,128)(2,1)S(1)}, bf16[4,32,1024]{2,1,0:T(8,128)(2,1)S(1)}, u32[]{:S(2)}, u32[]{:S(2)}) %collective-permute-start.5) | collective-permute-done | bytes 262176 | tf_op jit(solution)/shard_map/ppermute | solution.py:566
  22.5 0.7 collective-permute-done.4
  23.2 3.0 %collective-permute-done.3 = bf16[4,32,1024]{2,1,0:T(8,128)(2,1)S(1)} collective-permute-done((bf16[4,32,1024]{2,1,0:T(8,128)(2,1)S(1)}, bf16[4,32,1024]{2,1,0:T(8,128)(2,1)S(1)}, u32[]{:S(2)}, u32[]{:S(2)}) %collective-permute-start.3) | collective-permute-done | bytes 262176 | tf_op jit(solution)/shard_map/ppermute | solution.py:566
  26.2 0.1 pad_maximum_fusion.mine
  26.3 0.1 collective-permute-start.6
  26.4 2.6 %collective-permute-done.6.other = bf16[4,4,32,1024]{3,2,1,0:T(8,128)(2,1)S(1)} collective-permute-done((bf16[4,4,32,1024]{3,2,1,0:T(8,128)(2,1)S(1)}, bf16[4,4,32,1024]{3,2,1,0:T(8,128)(2,1)S(1)}, u32[]{:S(2)}, u32[]{:S(2)}) %collective-permute-start.6) | collective-permute-done | bytes 1048608 | tf_op jit(solution)/shard_map/ppermute | solution.py:571
  29.1 10.3 %shard_map.50 = (f32[2048,1024]{1,0:T(8,128)S(1)}, f32[32,8,128]{2,1,0:T(8,128)S(1)}, bf16[4,4,2,32,1024]{4,3,2,1,0:T(8,128)(2,1)}, bf16[1024,1024]{1,0:T(8,128)(2,1)}) custom-call(s32[3]{0:T(128)S(1)} %pad_add_fusion.at, bf16[4,4,32,1024]{3,2,1,0:T(8,128)(2,1)S(1)} %pad_maximum_fusion.mine, bf16[4,4,32,1024]{3,2,1,0:T(8,128)(2,1)S(1)} %collective-permute-done.6.other, ...), custom_call_target="tpu_custom_call" | custom-call | flops 4294967296 | bytes 20971520 | tf_op jit(solution)/shard_map/pallas_call | solution.py:169
  39.4 12.2 %all_to_all.20.norms = f32[32,8,128]{2,1,0:T(8,128)S(1)} all-to-all(f32[32,8,128]{2,1,0:T(8,128)S(1)} %get-tuple-element.36), channel_id=1, replica_groups=mesh['pts'=8,'cent'=32] {'cent'}, dimensions={0} | all-to-all | bytes 262144 | tf_op jit(solution)/shard_map/all_to_all | solution.py:583
  51.6 1.3 shard_map.51
  52.9 16.6 %all_to_all.21.freqs = f32[8,16,128]{2,1,0:T(8,128)S(1)} all-to-all(f32[8,16,128]{2,1,0:T(8,128)S(1)} %get-tuple-element.38), channel_id=1, replica_groups=mesh['pts'=8,'cent'=32] {'pts'}, dimensions={0} | all-to-all | bytes 131072 | tf_op jit(solution)/shard_map/all_to_all | solution.py:585
  69.6 4.0 %shard_map.52 = f32[32,16,128]{2,1,0:T(8,128)} custom-call(f32[8,16,128]{2,1,0:T(8,128)S(1)} %all_to_all.21.freqs, f32[8,128]{1,0:T(8,128)S(1)} %get-tuple-element.39.inv, f32[2048,1024]{1,0:T(8,128)S(1)} %get-tuple-element.37.kern), custom_call_target="tpu_custom_call" | custom-call | flops 12582912 | bytes 8388608 | tf_op jit(solution)/shard_map/pallas_call | solution.py:253
  73.5 5.0 %all-to-all-start.2 = ((f32[32,16,128]{2,1,0:T(8,128)}), f32[32,16,128]{2,1,0:T(8,128)S(1)}, u32[]{:S(2)}, u32[]{:S(2)}) async-start(f32[32,16,128]{2,1,0:T(8,128)} %shard_map.52), calls=%async_computation.2 | async-start | bytes 524288 | tf_op jit(solution)/shard_map/all_to_all | solution.py:587
  78.6 7.4 %all-to-all-done.2.dens = f32[32,16,128]{2,1,0:T(8,128)S(1)} async-done(((f32[32,16,128]{2,1,0:T(8,128)}), f32[32,16,128]{2,1,0:T(8,128)S(1)}, u32[]{:S(2)}, u32[]{:S(2)}) %all-to-all-start.2) | async-done | bytes 262176 | tf_op jit(solution)/shard_map/all_to_all | solution.py:587
  86.0 17.1 %shard_map.53 = (bf16[2048,1024]{1,0:T(8,128)(2,1)S(1)}, bf16[2048,1024]{1,0:T(8,128)(2,1)S(1)}, f32[8,1024]{1,0:T(8,128)S(1)}, f32[8,128]{1,0:T(8,128)S(1)}, f3...) custom-call(s32[1]{0:T(128)} %bitcast.z, ...), custom_call_target="tpu_custom_call" | custom-call | flops 8589934592 | bytes 31457280 | tf_op jit(solution)/shard_map/pallas_call | solution.py:374
  103.2 0.6 collective-permute-start.7
  103.8 2.7 %collective-permute-start.8 = (bf16[1040,128]{1,0:T(8,128)(2,1)S(1)}, bf16[1040,128]{1,0:T(8,128)(2,1)S(1)}, u32[]{:S(2)}, u32[]{:S(2)}) collective-permute-start(bf16[1040,128]{1,0:T(8,128)(2,1)S(1)} %get-tuple-element.46), channel_id=1, source_target_pairs={{0,224},{32,0},{64,32},{96,64},{128,96},{160,128},{192,160},{224,1... | collective-permute-start | bytes 798728 | tf_op jit(solution)/shard_map/ppermute | solution.py:591
  106.5 5.2 %shard_map.54.refs_0_ = bf16[32,32,1152]{2,1,0:T(8,128)(2,1)} custom-call(bf16[2048,1024]{1,0:T(8,128)(2,1)} %cent.7, bf16[2048,1024]{1,0:T(8,128)(2,1)S(1)} %get-tuple-element.41.hi, bf16[2048,1024]{1,0:T(8,128)(2,1)S(1)} %get-tuple-element.42.lo, f32[8,1024]{1,0:T(8,128)S(1)} %get-tuple-element.43.csum, bf16[1024,1024]{1,0:T(8,128)(2,1)} %bitcast.17), custom_call_target="tpu_custom_call" | custom-call | flops 2147483648 | bytes 9437184 | tf_op jit(solution)/shard_map/pallas_call | solution.py:506
  111.7 1.7 collective-permute-done.7.got_right
  113.4 0.0 collective-permute-done.8.got_left
  113.4 3.1 %shard_map.55 = (bf16[2064,128]{1,0:T(8,128)(2,1)S(1)}, bf16[2064,128]{1,0:T(8,128)(2,1)S(1)}) custom-call(s32[1]{0:T(128)} %bitcast.z, f32[8,2048,128]{2,1,0:T(8,128)} %get-tuple-element.48.g, f32[8,128]{1,0:T(8,128)S(1)} %get-tuple-element.49.kl, bf16[1040,128]{1,0:T(8,128)(2,1)S(1)} %collective-permute-done.7.got_right, ...), custom_call_target="tpu_custom_call" | custom-call | flops 41943040 | bytes 3145728 | tf_op jit(solution)/shard_map/pallas_call | solution.py:445
  116.5 0.1 collective-permute-start.9
  116.6 3.2 %collective-permute-start.10 = (bf16[2064,128]{1,0:T(8,128)(2,1)S(1)}, bf16[2064,128]{1,0:T(8,128)(2,1)S(1)}, u32[]{:S(2)}, u32[]{:S(2)}) collective-permute-start(bf16[2064,128]{1,0:T(8,128)(2,1)S(1)} %get-tuple-element.56), channel_id=1, source_target_pairs={{0,224},{32,0},{64,32},{96,64},{128,96},{160,128},{192,160},{224,1... | collective-permute-start | bytes 1585160 | tf_op jit(solution)/shard_map/ppermute | solution.py:591
  119.8 11.1 %shard_map.56 = bf16[32,32,1152]{2,1,0:T(8,128)(2,1)} custom-call(bf16[2048,1024]{1,0:T(8,128)(2,1)} %cent.7, bf16[2048,1024]{1,0:T(8,128)(2,1)S(1)} %get-tuple-element.41.hi, bf16[2048,1024]{1,0:T(8,128)(2,1)S(1)} %get-tuple-element.42.lo, f32[8,1024]{1,0:T(8,128)S(1)} %get-tuple-element.43.csum, ...), custom_call_target="tpu_custom_call", output_to_operand_aliasing={{}: (5, {})} | custom-call | flops 6442450944 | bytes 9437184 | tf_op jit(solution)/shard_map/pallas_call | solution.py:506
  130.9 0.7 collective-permute-done.9.got_right
  131.5 4.9 %all-to-all-start.3 = ((bf16[32,32,1152]{2,1,0:T(8,128)(2,1)}), bf16[32,32,1152]{2,1,0:T(8,128)(2,1)S(1)}, u32[]{:S(2)}, u32[]{:S(2)}) async-start(bf16[32,32,1152]{2,1,0:T(8,128)(2,1)} %shard_map.56), calls=%async_computation.3 | async-start | bytes 4718592 | tf_op jit(solution)/shard_map/all_to_all | solution.py:603
  136.4 3.1 %shard_map.58 = (bf16[2064,128]{1,0:T(8,128)(2,1)S(1)}, bf16[2064,128]{1,0:T(8,128)(2,1)S(1)}) custom-call(s32[1]{0:T(128)} %bitcast.z, f32[8,2048,128]{2,1,0:T(8,128)} %get-tuple-element.48.g, f32[8,128]{1,0:T(8,128)S(1)} %get-tuple-element.49.kl, bf16[2064,128]{1,0:T(8,128)(2,1)S(1)} %collective-permute-done.9.got_right, ...), custom_call_target="tpu_custom_call" | custom-call | flops 41943040 | bytes 3145728 | tf_op jit(solution)/shard_map/pallas_call | solution.py:445
  139.6 0.1 collective-permute-start.11
  139.6 3.2 %collective-permute-start.12 = (bf16[2064,128]{1,0:T(8,128)(2,1)S(1)}, bf16[2064,128]{1,0:T(8,128)(2,1)S(1)}, u32[]{:S(2)}, u32[]{:S(2)}) collective-permute-start(bf16[2064,128]{1,0:T(8,128)(2,1)S(1)} %get-tuple-element.61), channel_id=1, source_target_pairs={{0,224},{32,0},{64,32},{96,64},{128,96},{160,128},{192,160},{224,1... | collective-permute-start | bytes 1585160 | tf_op jit(solution)/shard_map/ppermute | solution.py:591
  142.9 12.0 %collective-permute-done.11.got_right = bf16[2064,128]{1,0:T(8,128)(2,1)S(1)} collective-permute-done((bf16[2064,128]{1,0:T(8,128)(2,1)S(1)}, bf16[2064,128]{1,0:T(8,128)(2,1)S(1)}, u32[]{:S(2)}, u32[]{:S(2)}) %collective-permute-start.11) | collective-permute-done | bytes 528416 | tf_op jit(solution)/shard_map/ppermute | solution.py:591
  154.9 3.9 %shard_map.59 = (bf16[2064,128]{1,0:T(8,128)(2,1)}, bf16[2064,128]{1,0:T(8,128)(2,1)}) custom-call(s32[1]{0:T(128)} %bitcast.z, f32[8,2048,128]{2,1,0:T(8,128)} %get-tuple-element.48.g, f32[8,128]{1,0:T(8,128)S(1)} %get-tuple-element.49.kl, bf16[2064,128]{1,0:T(8,128)(2,1)S(1)} %collective-permute-done.11.got_right, ...), custom_call_target="tpu_custom_call" | custom-call | flops 41943040 | bytes 3145728 | tf_op jit(solution)/shard_map/pallas_call | solution.py:445
  158.8 0.1 collective-permute-start.13
  158.9 3.4 %collective-permute-start.14 = (bf16[2064,128]{1,0:T(8,128)(2,1)}, bf16[2064,128]{1,0:T(8,128)(2,1)S(1)}, u32[]{:S(2)}, u32[]{:S(2)}) collective-permute-start(bf16[2064,128]{1,0:T(8,128)(2,1)} %get-tuple-element.63), channel_id=1, source_target_pairs={{0,224},{32,0},{64,32},{96,64},{128,96},{160,128},{192,160},{224,1... | collective-permute-start | bytes 1585160 | tf_op jit(solution)/shard_map/ppermute | solution.py:591
  162.3 4.4 %all-to-all-done.3.msgs = bf16[32,32,1152]{2,1,0:T(8,128)(2,1)S(1)} async-done(((bf16[32,32,1152]{2,1,0:T(8,128)(2,1)}), bf16[32,32,1152]{2,1,0:T(8,128)(2,1)S(1)}, u32[]{:S(2)}, u32[]{:S(2)}) %all-to-all-start.3) | async-done | bytes 2359328 | tf_op jit(solution)/shard_map/all_to_all | solution.py:603
  166.6 3.0 %shard_map.57 = f32[32,1024]{1,0:T(8,128)} custom-call(bf16[32,32,1152]{2,1,0:T(8,128)(2,1)S(1)} %all-to-all-done.3.msgs), custom_call_target="tpu_custom_call" | custom-call | flops 20971520 | bytes 3145728 | tf_op jit(solution)/shard_map/pallas_call | solution.py:535
  169.7 3.9 %collective-permute-done.13.right = bf16[2064,128]{1,0:T(8,128)(2,1)S(1)} collective-permute-done((bf16[2064,128]{1,0:T(8,128)(2,1)}, bf16[2064,128]{1,0:T(8,128)(2,1)S(1)}, u32[]{:S(2)}, u32[]{:S(2)}) %collective-permute-start.13) | collective-permute-done | bytes 528416 | tf_op jit(solution)/shard_map/ppermute | solution.py:591
  173.5 2.6 %shard_map.60 = (f32[2048,128]{1,0:T(8,128)}, f32[1,1]{1,0:T(1,128)}) custom-call(s32[1]{0:T(128)} %bitcast.z, f32[8,2048,128]{2,1,0:T(8,128)} %get-tuple-element.48.g, f32[8,128]{1,0:T(8,128)S(1)} %get-tuple-element.49.kl, bf16[2064,128]{1,0:T(8,128)(2,1)S(1)} %collective-permute-done.13.right, bf16[2064,128]{1,0:T(8,128)(2,1)S(1)} %collective-permute-done.14.left), custom_call_target="tpu_custom_call" | custom-call | flops 20971520 | bytes 4194304 | tf_op jit(solution)/shard_map/pallas_call | solution.py:475
  (8 shorter events, 0.0 us)
Async XLA Ops:
  0.6 5.1 %collective-permute-start.2 = (bf16[32,1024]{1,0:T(8,128)(2,1)}, bf16[32,1024]{1,0:T(8,128)(2,1)S(1)}, u32[]{:S(2)}, u32[]{:S(2)}) collective-permute-start(bf16[32,1024]{1,0:T(8,128)(2,1)} %bitcast.13), channel_id=1, source_target_pairs={{0,6},{1,7},{2,0},{3,1},{4,2},{5,3},{6,4},{7,5},{8,14},{9,15},{10,... | collective-permute-start | bytes 196616 | tf_op jit(solution)/shard_map/ppermute | solution.py:566
  2.9 6.0 %collective-permute-start.1 = (bf16[32,1024]{1,0:T(8,128)(2,1)}, bf16[32,1024]{1,0:T(8,128)(2,1)S(1)}, u32[]{:S(2)}, u32[]{:S(2)}) collective-permute-start(bf16[32,1024]{1,0:T(8,128)(2,1)} %bitcast.14), channel_id=1, source_target_pairs={{0,4},{1,5},{2,6},{3,7},{4,0},{5,1},{6,2},{7,3},{8,12},{9,13},{10,... | collective-permute-start | bytes 196616 | tf_op jit(solution)/shard_map/ppermute | solution.py:566
  3.7 5.1 %collective-permute-start = (bf16[32,1024]{1,0:T(8,128)(2,1)}, bf16[32,1024]{1,0:T(8,128)(2,1)S(1)}, u32[]{:S(2)}, u32[]{:S(2)}) collective-permute-start(bf16[32,1024]{1,0:T(8,128)(2,1)} %bitcast.15), channel_id=1, source_target_pairs={{0,2},{1,3},{2,4},{3,5},{4,6},{5,7},{6,0},{7,1},{8,10},{9,11},{10,... | collective-permute-start | bytes 196616 | tf_op jit(solution)/shard_map/ppermute | solution.py:566
  8.9 0.8 copy-start.1
  10.3 12.2 %collective-permute-start.5 = (bf16[4,32,1024]{2,1,0:T(8,128)(2,1)S(1)}, bf16[4,32,1024]{2,1,0:T(8,128)(2,1)S(1)}, u32[]{:S(2)}, u32[]{:S(2)}) collective-permute-start(bf16[4,32,1024]{2,1,0:T(8,128)(2,1)S(1)} %shard_map.49), channel_id=1, source_target_pairs={{0,24},{1,25},{2,26},{3,27},{4,28},{5,29},{6,30},{7,31},{8,0},{9,1... | collective-permute-start | bytes 786440 | tf_op jit(solution)/shard_map/ppermute | solution.py:566
  12.5 10.7 %collective-permute-start.4 = (bf16[4,32,1024]{2,1,0:T(8,128)(2,1)S(1)}, bf16[4,32,1024]{2,1,0:T(8,128)(2,1)S(1)}, u32[]{:S(2)}, u32[]{:S(2)}) collective-permute-start(bf16[4,32,1024]{2,1,0:T(8,128)(2,1)S(1)} %shard_map.49), channel_id=1, source_target_pairs={{0,16},{1,17},{2,18},{3,19},{4,20},{5,21},{6,22},{7,23},{8,24},{9,... | collective-permute-start | bytes 786440 | tf_op jit(solution)/shard_map/ppermute | solution.py:566
  13.3 12.9 %collective-permute-start.3 = (bf16[4,32,1024]{2,1,0:T(8,128)(2,1)S(1)}, bf16[4,32,1024]{2,1,0:T(8,128)(2,1)S(1)}, u32[]{:S(2)}, u32[]{:S(2)}) collective-permute-start(bf16[4,32,1024]{2,1,0:T(8,128)(2,1)S(1)} %shard_map.49), channel_id=1, source_target_pairs={{0,8},{1,9},{2,10},{3,11},{4,12},{5,13},{6,14},{7,15},{8,16},{9,17... | collective-permute-start | bytes 786440 | tf_op jit(solution)/shard_map/ppermute | solution.py:566
  26.3 2.7 %collective-permute-start.6 = (bf16[4,4,32,1024]{3,2,1,0:T(8,128)(2,1)S(1)}, bf16[4,4,32,1024]{3,2,1,0:T(8,128)(2,1)S(1)}, u32[]{:S(2)}, u32[]{:S(2)}) collective-permute-start(bf16[4,4,32,1024]{3,2,1,0:T(8,128)(2,1)S(1)} %pad_maximum_fusion.mine), channel_id=1, source_target_pairs={{0,1},{1,0},{2,3},{3,2},{4,5},{5,4},{6,7},{7,6},{8,9},{9,8},{10,11... | collective-permute-start | bytes 3145736 | tf_op jit(solution)/shard_map/ppermute | solution.py:571
  39.4 30.2 %copy-start = (f32[2048,1024]{1,0:T(8,128)}, f32[2048,1024]{1,0:T(8,128)S(1)}, u32[]{:S(2)}) copy-start(f32[2048,1024]{1,0:T(8,128)S(1)} %get-tuple-element.37.kern) | copy-start | bytes 25165828
  69.6 16.5 %copy-start.2 = (bf16[1024,1024]{1,0:T(8,128)(2,1)S(1)}, bf16[1024,1024]{1,0:T(8,128)(2,1)}, u32[]{:S(2)}) copy-start(bf16[1024,1024]{1,0:T(8,128)(2,1)} %get-tuple-element.40.zn_hbm) | copy-start | bytes 6291460
  73.5 12.5 %all-to-all-start.2 = ((f32[32,16,128]{2,1,0:T(8,128)}), f32[32,16,128]{2,1,0:T(8,128)S(1)}, u32[]{:S(2)}, u32[]{:S(2)}) async-start(f32[32,16,128]{2,1,0:T(8,128)} %shard_map.52), calls=%async_computation.2 | async-start | bytes 524288 | tf_op jit(solution)/shard_map/all_to_all | solution.py:587
  103.2 10.2 %collective-permute-start.7 = (bf16[1040,128]{1,0:T(8,128)(2,1)S(1)}, bf16[1040,128]{1,0:T(8,128)(2,1)S(1)}, u32[]{:S(2)}, u32[]{:S(2)}) collective-permute-start(bf16[1040,128]{1,0:T(8,128)(2,1)S(1)} %get-tuple-element.45), channel_id=1, source_target_pairs={{0,32},{32,64},{64,96},{96,128},{128,160},{160,192},{192,224},{224... | collective-permute-start | bytes 798728 | tf_op jit(solution)/shard_map/ppermute | solution.py:591
  103.8 9.6 %collective-permute-start.8 = (bf16[1040,128]{1,0:T(8,128)(2,1)S(1)}, bf16[1040,128]{1,0:T(8,128)(2,1)S(1)}, u32[]{:S(2)}, u32[]{:S(2)}) collective-permute-start(bf16[1040,128]{1,0:T(8,128)(2,1)S(1)} %get-tuple-element.46), channel_id=1, source_target_pairs={{0,224},{32,0},{64,32},{96,64},{128,96},{160,128},{192,160},{224,1... | collective-permute-start | bytes 798728 | tf_op jit(solution)/shard_map/ppermute | solution.py:591
  116.5 15.1 %collective-permute-start.9 = (bf16[2064,128]{1,0:T(8,128)(2,1)S(1)}, bf16[2064,128]{1,0:T(8,128)(2,1)S(1)}, u32[]{:S(2)}, u32[]{:S(2)}) collective-permute-start(bf16[2064,128]{1,0:T(8,128)(2,1)S(1)} %get-tuple-element.55), channel_id=1, source_target_pairs={{0,32},{32,64},{64,96},{96,128},{128,160},{160,192},{192,224},{224... | collective-permute-start | bytes 1585160 | tf_op jit(solution)/shard_map/ppermute | solution.py:591
  116.6 15.0 %collective-permute-start.10 = (bf16[2064,128]{1,0:T(8,128)(2,1)S(1)}, bf16[2064,128]{1,0:T(8,128)(2,1)S(1)}, u32[]{:S(2)}, u32[]{:S(2)}) collective-permute-start(bf16[2064,128]{1,0:T(8,128)(2,1)S(1)} %get-tuple-element.56), channel_id=1, source_target_pairs={{0,224},{32,0},{64,32},{96,64},{128,96},{160,128},{192,160},{224,1... | collective-permute-start | bytes 1585160 | tf_op jit(solution)/shard_map/ppermute | solution.py:591
  131.5 35.1 %all-to-all-start.3 = ((bf16[32,32,1152]{2,1,0:T(8,128)(2,1)}), bf16[32,32,1152]{2,1,0:T(8,128)(2,1)S(1)}, u32[]{:S(2)}, u32[]{:S(2)}) async-start(bf16[32,32,1152]{2,1,0:T(8,128)(2,1)} %shard_map.56), calls=%async_computation.3 | async-start | bytes 4718592 | tf_op jit(solution)/shard_map/all_to_all | solution.py:603
  139.6 15.4 %collective-permute-start.11 = (bf16[2064,128]{1,0:T(8,128)(2,1)S(1)}, bf16[2064,128]{1,0:T(8,128)(2,1)S(1)}, u32[]{:S(2)}, u32[]{:S(2)}) collective-permute-start(bf16[2064,128]{1,0:T(8,128)(2,1)S(1)} %get-tuple-element.60), channel_id=1, source_target_pairs={{0,32},{32,64},{64,96},{96,128},{128,160},{160,192},{192,224},{224... | collective-permute-start | bytes 1585160 | tf_op jit(solution)/shard_map/ppermute | solution.py:591
  139.6 15.3 %collective-permute-start.12 = (bf16[2064,128]{1,0:T(8,128)(2,1)S(1)}, bf16[2064,128]{1,0:T(8,128)(2,1)S(1)}, u32[]{:S(2)}, u32[]{:S(2)}) collective-permute-start(bf16[2064,128]{1,0:T(8,128)(2,1)S(1)} %get-tuple-element.61), channel_id=1, source_target_pairs={{0,224},{32,0},{64,32},{96,64},{128,96},{160,128},{192,160},{224,1... | collective-permute-start | bytes 1585160 | tf_op jit(solution)/shard_map/ppermute | solution.py:591
  158.8 14.7 %collective-permute-start.13 = (bf16[2064,128]{1,0:T(8,128)(2,1)}, bf16[2064,128]{1,0:T(8,128)(2,1)S(1)}, u32[]{:S(2)}, u32[]{:S(2)}) collective-permute-start(bf16[2064,128]{1,0:T(8,128)(2,1)} %get-tuple-element.62), channel_id=1, source_target_pairs={{0,32},{32,64},{64,96},{96,128},{128,160},{160,192},{192,224},{224... | collective-permute-start | bytes 1585160 | tf_op jit(solution)/shard_map/ppermute | solution.py:591
  158.9 14.6 %collective-permute-start.14 = (bf16[2064,128]{1,0:T(8,128)(2,1)}, bf16[2064,128]{1,0:T(8,128)(2,1)S(1)}, u32[]{:S(2)}, u32[]{:S(2)}) collective-permute-start(bf16[2064,128]{1,0:T(8,128)(2,1)} %get-tuple-element.63), channel_id=1, source_target_pairs={{0,224},{32,0},{64,32},{96,64},{128,96},{160,128},{192,160},{224,1... | collective-permute-start | bytes 1585160 | tf_op jit(solution)/shard_map/ppermute | solution.py:591
